TPU v7x, 32 devices: a whole 2x2x4 slice. The times are simulated.
32 devices in a mesh: run: 2 (over y), gy: 4 (over z), gx: 2 (over x), gz: 2 (over core).
Axes of the slice: x: 2, y: 2, z: 4, core: 2. Of those that a mesh axis runs over, the one named last changes fastest.
Arguments:
- facies: int32 [64, 128, 256], P(('run', 'gx'), 'gy', 'gz'), parts along dimension 0, may hold values from 0 to 4
- pressure_old: float32 [64, 128, 256], P(('run', 'gx'), 'gy', 'gz'), parts along dimension 0, may hold values from -6 to 6
- saturation: float32 [32, 64, 128], P(('run', 'gx'), 'gy', 'gz'), parts along dimension 0, may hold values from 0 to 1
- well_x: int32 [128], P('run'), parts along dimension 0, may hold values from 0 to 31
- well_y: int32 [128], P('run'), parts along dimension 0, may hold values from 0 to 127
- well_rate: int32 [128], P('run'), parts along dimension 0, may hold values from 1 to 64
- enc_first: bfloat16 [16, 4, 3, 3, 3], replicated, may hold values from -0.625 to 0.625
- enc_second: bfloat16 [16, 16, 3, 3, 3], replicated, may hold values from -0.3125 to 0.3125
- mid_first: bfloat16 [16, 16, 3, 3, 3], replicated, may hold values from -0.3125 to 0.3125
- mid_second: bfloat16 [16, 16, 3, 3, 3], replicated, may hold values from -0.3125 to 0.3125
- dec_weight: bfloat16 [16, 32, 3, 3, 3], replicated, may hold values from -0.21875 to 0.21875
- head_weight: bfloat16 [16], replicated, may hold values from -1.5 to 1.5
Outputs:
- pressure: float32 [64, 128, 256], P(('run', 'gx'), 'gy', 'gz'), parts along dimension 0
- saturation_new: float32 [32, 64, 128], P(('run', 'gx'), 'gy', 'gz'), parts along dimension 0
There are 2 independent parts, one for each index of `run`. A program takes and returns all parts, laid end to end along the dimension named above; an argument that names none is the same for every part. Nothing has to cross between parts.
Inputs may be any that keep to these rules, and one draw needn't show every extreme that they name: facies classes index the tables.
All inputs are finite; a program needn't handle non-finite values.
Results may differ from a plain program's by a relative error of at most 0.0035.
Values may be sent and summed in bfloat16 or wider, within the bound.
A program may use at most 192 MiB of HBM per device.

v0:
```python
import jax
import jax.numpy as jnp
from jax import lax
from jax.sharding import PartitionSpec as P

COARSE_SWEEPS = 8


PERM_TABLE = (0.02, 0.15, 0.8, 2.5, 9.0)
LOG_PERM_TABLE = (-3.912023, -1.89712, -0.223144, 0.916291, 2.197225)
PORE_TABLE = (0.05, 0.12, 0.2, 0.25, 0.3)
storage_factor = 0.0002
vertical_factor = 0.5
relax_weight = 0.6666667
rate_unit = 0.05


def with_halo(block, sides, width):
    for axis, dim in sides:
        count = lax.axis_size(axis)
        forward = [(i, i + 1) for i in range(count - 1)]
        backward = [(target, source) for source, target in forward]
        low = lax.ppermute(
            lax.slice_in_dim(block, block.shape[dim] - width, None, axis=dim), axis, forward
        )
        high = lax.ppermute(lax.slice_in_dim(block, 0, width, axis=dim), axis, backward)
        block = jnp.concatenate([low, block, high], axis=dim)
    return block


def table_lookup(facies, table):
    result = jnp.zeros(facies.shape, jnp.float32)
    for entry_index in range(len(table)):
        result = result + jnp.where(
            facies == entry_index, jnp.float32(table[entry_index]), jnp.float32(0.0)
        )
    return result


def harmonic(lower, upper):
    return 2.0 * lower * upper / (lower + upper)


def with_diagonal(storage, faces):
    diagonal = storage + faces[0] + faces[1] + faces[2] + faces[3] + faces[4] + faces[5]
    return (storage, faces, diagonal)


def fine_operator(permeability, padded, storage):
    faces = (
        harmonic(padded[:-2, 1:-1, 1:-1], permeability),
        harmonic(permeability, padded[2:, 1:-1, 1:-1]),
        harmonic(padded[1:-1, :-2, 1:-1], permeability),
        harmonic(permeability, padded[1:-1, 2:, 1:-1]),
        vertical_factor * harmonic(padded[1:-1, 1:-1, :-2], permeability),
        vertical_factor * harmonic(permeability, padded[1:-1, 1:-1, 2:]),
    )
    return with_diagonal(storage, faces)


def pair_yz(values):
    size_x, size_y, size_z = values.shape
    return values.reshape(size_x, size_y // 2, 2, size_z // 2, 2).sum(axis=(2, 4))


def pair_xz(values):
    size_x, size_y, size_z = values.shape
    return values.reshape(size_x // 2, 2, size_y, size_z // 2, 2).sum(axis=(1, 4))


def pair_xy(values):
    size_x, size_y, size_z = values.shape
    return values.reshape(size_x // 2, 2, size_y // 2, 2, size_z).sum(axis=(1, 3))


def block_sum(values):
    size_x, size_y, size_z = values.shape
    return values.reshape(size_x // 2, 2, size_y // 2, 2, size_z // 2, 2).sum(axis=(1, 3, 5))


def coarsen_operator(operator):
    storage, faces, diagonal = operator
    new_faces = (
        pair_yz(faces[0][0::2]),
        pair_yz(faces[1][1::2]),
        pair_xz(faces[2][:, 0::2]),
        pair_xz(faces[3][:, 1::2]),
        pair_xy(faces[4][:, :, 0::2]),
        pair_xy(faces[5][:, :, 1::2]),
    )
    return with_diagonal(block_sum(storage), new_faces)


def apply_padded(field, padded, operator):
    storage, faces, diagonal = operator
    beside = faces[0] * padded[:-2, 1:-1, 1:-1] + faces[1] * padded[2:, 1:-1, 1:-1]
    beside = beside + faces[2] * padded[1:-1, :-2, 1:-1] + faces[3] * padded[1:-1, 2:, 1:-1]
    beside = beside + faces[4] * padded[1:-1, 1:-1, :-2] + faces[5] * padded[1:-1, 1:-1, 2:]
    return diagonal * field - beside


def apply_level(field, operator):
    padded = with_halo(field, (("gy", 1), ("gx", 0), ("gz", 2)), 1)
    return apply_padded(field, padded, operator)


def relax(field, rhs, operator):
    return field + relax_weight * (rhs - apply_level(field, operator)) / operator[2]


def enlarge(values):
    return jnp.repeat(jnp.repeat(jnp.repeat(values, 2, 0), 2, 1), 2, 2)


def enlarge_channels(values):
    return jnp.repeat(jnp.repeat(jnp.repeat(values, 2, 1), 2, 2), 2, 3)


def well_columns(well_x, well_y, well_rate, start_x, start_y, count_x, count_y):
    along_x = (well_x[:, None] == start_x + jnp.arange(count_x, dtype=jnp.int32)[None, :]).astype(
        jnp.float32
    )
    along_y = (well_y[:, None] == start_y + jnp.arange(count_y, dtype=jnp.int32)[None, :]).astype(
        jnp.float32
    )
    weighted = along_x * well_rate.astype(jnp.float32)[:, None]
    return jnp.dot(weighted.T, along_y, precision=lax.Precision.HIGHEST)


def pool_mean(values):
    channels, size_x, size_y, size_z = values.shape
    summed = (
        values.astype(jnp.float32)
        .reshape(channels, size_x // 2, 2, size_y // 2, 2, size_z // 2, 2)
        .sum(axis=(2, 4, 6))
    )
    return (summed * 0.125).astype(jnp.bfloat16)


def conv_valid(padded, weight):
    in_channels = padded.shape[0]
    out_x, out_y, out_z = (padded.shape[1] - 2, padded.shape[2] - 2, padded.shape[3] - 2)
    pieces = []
    for shift_x in range(3):
        for shift_y in range(3):
            for shift_z in range(3):
                pieces.append(
                    padded[
                        :,
                        shift_x : shift_x + out_x,
                        shift_y : shift_y + out_y,
                        shift_z : shift_z + out_z,
                    ]
                )
    patches = jnp.stack(pieces, axis=1).reshape(in_channels * 27, out_x * out_y * out_z)
    matrix = weight.reshape(weight.shape[0], in_channels * 27)
    result = jnp.dot(matrix, patches, preferred_element_type=jnp.float32)
    return result.reshape(weight.shape[0], out_x, out_y, out_z)


def silu_layer(padded, weight):
    return jax.nn.silu(conv_valid(padded, weight)).astype(jnp.bfloat16)


def unet_rim(values):
    return with_halo(values, (("gy", 2), ("gx", 1), ("gz", 3)), 1)


def pooled_edge(values):
    return with_halo(values, (("gy", 2), ("gx", 1), ("gz", 3)), 1)


def on_device(
    facies,
    pressure_old,
    saturation,
    well_x,
    well_y,
    well_rate,
    enc_first,
    enc_second,
    mid_first,
    mid_second,
    dec_weight,
    head_weight,
):
    size_x, size_y, size_z = facies.shape
    permeability = table_lookup(facies, PERM_TABLE)
    storage = storage_factor * table_lookup(facies, PORE_TABLE)
    padded_perm = with_halo(permeability, (("gy", 1), ("gx", 0), ("gz", 2)), 1)
    level_zero = fine_operator(permeability, padded_perm, storage)
    column = well_columns(
        well_x,
        well_y,
        well_rate,
        lax.axis_index("gx") * size_x,
        lax.axis_index("gy") * size_y,
        size_x,
        size_y,
    )
    source = jnp.broadcast_to(rate_unit * column[:, :, None], facies.shape)
    rhs = storage * pressure_old + source
    state_zero = relax(pressure_old, rhs, level_zero)
    rhs_one = block_sum(rhs - apply_level(state_zero, level_zero))
    level_one = coarsen_operator(level_zero)
    level_two = coarsen_operator(level_one)
    level_three = coarsen_operator(level_two)
    state_one = relax_weight * rhs_one / level_one[2]
    rhs_two = block_sum(rhs_one - apply_level(state_one, level_one))
    state_two = relax_weight * rhs_two / level_two[2]
    rhs_three = block_sum(rhs_two - apply_level(state_two, level_two))
    state_three = relax_weight * rhs_three / level_three[2]
    for sweep_turn in range(COARSE_SWEEPS - 1):
        padded_coarse = with_halo(state_three, (("gy", 1), ("gx", 0), ("gz", 2)), 1)
        state_three = (
            state_three
            + relax_weight
            * (rhs_three - apply_padded(state_three, padded_coarse, level_three))
            / level_three[2]
        )
    state_two = relax(state_two + enlarge(state_three), rhs_two, level_two)
    state_one = relax(state_one + enlarge(state_two), rhs_one, level_one)
    pressure = relax(state_zero + enlarge(state_one), rhs, level_zero)
    mean_pressure = block_sum(pressure) * 0.125
    mean_logperm = block_sum(table_lookup(facies, LOG_PERM_TABLE)) * 0.125
    mean_source = block_sum(source) * 0.125
    features = jnp.stack([saturation, mean_pressure, mean_logperm, mean_source]).astype(
        jnp.bfloat16
    )
    first = silu_layer(unet_rim(features), enc_first)
    skip = silu_layer(unet_rim(first), enc_second)
    pooled = pool_mean(skip)
    middle = silu_layer(pooled_edge(pooled), mid_first)
    deep = silu_layer(pooled_edge(middle), mid_second)
    joined = with_halo(
        jnp.concatenate([skip, enlarge_channels(deep)], 0), (("gy", 2), ("gx", 1), ("gz", 3)), 1
    )
    decoded = silu_layer(joined, dec_weight)
    channels = decoded.shape[0]
    delta = jnp.dot(
        head_weight[None, :], decoded.reshape(channels, -1), preferred_element_type=jnp.float32
    )
    return (pressure, saturation + delta.reshape(saturation.shape))


def solution(mesh):
    return jax.shard_map(
        on_device,
        mesh=mesh,
        in_specs=(
            P(("run", "gx"), "gy", "gz"),
            P(("run", "gx"), "gy", "gz"),
            P(("run", "gx"), "gy", "gz"),
            P("run"),
            P("run"),
            P("run"),
            P(),
            P(),
            P(),
            P(),
            P(),
            P(),
        ),
        out_specs=(P(("run", "gx"), "gy", "gz"), P(("run", "gx"), "gy", "gz")),
        check_vma=False,
    )
```

profile of v0, /device:TPU:0, one launch (start us, length us, event | category | flops | bytes accessed | tf_op | source)
XLA Modules:
  0.0 881.2 jit_solution(9289372720337374992)
XLA Ops:
  2.9 5.6 collective-permute-start.6
  11.9 4.6 collective-permute-start
  19.2 4.5 collective-permute-start.8
  40.1 4.6 collective-permute-start.12
  47.3 4.5 collective-permute-start.14
  55.7 5.0 collective-permute-start.16
  60.7 6.4 slice.1335
  67.1 6.3 slice.1334
  83.4 18.2 %reshape.362 = f32[8,2,16,2,64,2]{5,4,3,2,1,0:T(8,128)} reshape(f32[16,32,128]{2,1,0:T(8,128)S(1)} %get-tuple-element.15) | data formatting | bytes 524288 | tf_op jit(solution)/shard_map/reshape | solution.py:78
  101.6 7.7 reduce_sum.253
  117.8 18.1 %reshape.361 = f32[8,2,16,2,64,2]{5,4,3,2,1,0:T(8,128)} reshape(f32[16,32,128]{2,1,0:T(8,128)S(1)} %fusion.36) | data formatting | bytes 524288 | tf_op jit(solution)/shard_map/reshape | solution.py:78
  135.9 7.1 reduce_sum.252
  145.0 4.8 collective-permute-start.18
  153.6 5.7 collective-permute-start.20
  179.2 4.7 collective-permute-start.22
  202.5 4.8 collective-permute-start.24
  210.0 4.5 collective-permute-start.26
  224.4 4.8 collective-permute-start.30
  231.8 4.5 collective-permute-start.32
  243.6 4.8 collective-permute-start.36
  251.0 4.5 collective-permute-start.38
  262.8 4.8 collective-permute-start.42
  270.2 4.5 collective-permute-start.44
  282.0 4.8 collective-permute-start.48
  289.4 4.5 collective-permute-start.50
  301.2 4.8 collective-permute-start.54
  308.6 4.5 collective-permute-start.56
  320.3 4.8 collective-permute-start.60
  327.8 4.5 collective-permute-start.62
  339.5 4.8 collective-permute-start.66
  346.9 4.5 collective-permute-start.68
  358.9 4.8 collective-permute-start.72
  366.4 4.5 collective-permute-start.74
  378.7 4.8 collective-permute-start.78
  386.2 4.5 collective-permute-start.80
  400.2 4.8 collective-permute-start.84
  407.9 4.4 collective-permute-start.86
  412.4 18.1 %reshape.395 = f32[8,2,16,2,64,2]{5,4,3,2,1,0:T(8,128)} reshape(f32[16,32,128]{2,1,0:T(8,128)S(1)} %copy-done.60) | data formatting | bytes 524288 | tf_op jit(solution)/shard_map/reshape | solution.py:78
  430.5 7.1 reduce_sum.277
  444.1 18.1 %reshape.394 = f32[8,2,16,2,64,2]{5,4,3,2,1,0:T(8,128)} reshape(f32[16,32,128]{2,1,0:T(8,128)S(1)} %fusion.23) | data formatting | bytes 524288 | tf_op jit(solution)/shard_map/reshape | solution.py:78
  462.2 7.0 reduce_sum.276
  470.6 4.8 collective-permute-start.90
  478.2 4.5 collective-permute-start.92
  509.8 5.1 reshape.396
  517.4 4.8 collective-permute-start.96
  525.7 4.6 collective-permute-start.98
  550.1 4.3 fusion.10
  585.4 19.0 %reshape.400 = bf16[432,8192]{1,0:T(8,128)(2,1)} reshape(bf16[16,27,8,16,64]{4,3,2,1,0:T(8,128)(2,1)} %copy_dynamic-update-slice_fusion.28) | data formatting | bytes 14155776 | tf_op jit(solution)/shard_map/reshape | solution.py:155
  604.4 4.1 convolution_bitcast_fusion
  611.1 5.7 copy.1572
  619.2 4.9 collective-permute-start.102
  627.0 4.6 collective-permute-start.104
  660.1 8.7 copy.1574
  668.8 4.6 reshape.404
  676.5 4.6 collective-permute-start.108
  685.3 4.5 collective-permute-start.110
  718.5 5.3 reshape.408
  731.1 4.6 collective-permute-start.114
  740.0 4.8 collective-permute-start.116
  768.4 3.8 slice_bitcast_fusion
  775.7 10.3 %fusion.1 = (bf16[32,1,8,16,64]{4,0,3,2,1:T(8,128)(2,1)}, bf16[32,1,8,16,64]{4,0,3,2,1:T(8,128)(2,1)S(1)}, bf16[32,1,8,16,64]{4,0,3,2,1:T(8,128)(2,1)}, bf16[32,...) fusion(bf16[32,10,18,64]{3,0,2,1:T(8,128)(2,1)} %copy.1617, ...), kind=kLoop, calls=%fused_computation.18 | loop fusion | flops 9437184 | bytes 5467392 | tf_op jit(solution)/shard_map/stack | solution.py:155
  789.7 9.6 %fusion = (bf16[32,1,8,16,64]{4,0,3,2,1:T(8,128)(2,1)S(1)}, bf16[32,1,8,16,64]{4,0,3,2,1:T(8,128)(2,1)S(1)}, bf16[32,1,8,16,64]{4,0,3,2,1:T(8,128)(2,1)S(1)}, bf...) fusion(bf16[32,10,18,1]{3,0,2,1:T(8,128)(2,1)} %copy.1621, ...), kind=kLoop, calls=%fused_computation.15 | loop fusion | flops 9437184 | bytes 5467392 | tf_op jit(solution)/shard_map/stack | solution.py:155
  835.3 36.9 %reshape.414 = bf16[864,8192]{1,0:T(8,128)(2,1)} reshape(bf16[32,27,8,16,64]{4,3,2,1,0:T(8,128)(2,1)} %copy_dynamic-update-slice_fusion) | data formatting | bytes 28311552 | tf_op jit(solution)/shard_map/reshape | solution.py:155
  872.3 7.1 multiply_convert_fusion.3
  (849 shorter events, 444.6 us)
Async XLA Ops:
  1.6 15.5 %collective-permute-start.7 = (f32[16,1,128]{2,1,0:T(1,128)S(1)}, f32[16,1,128]{2,1,0:T(1,128)S(1)}, u32[]{:S(2)}, u32[]{:S(2)}) collective-permute-start(f32[16,1,128]{2,1,0:T(1,128)S(1)} %get-tuple-element.127), channel_id=1, source_target_pairs={{4,0},{8,4},{12,8},{5,1},{9,5},{13,9},{6,2},{10,6},{14,10},{7,3},{... | collective-permute-start | bytes 24584 | tf_op jit(solution)/shard_map/ppermute | solution.py:26
  2.9 14.2 %collective-permute-start.6 = (f32[16,1,128]{2,1,0:T(1,128)S(1)}, f32[16,1,128]{2,1,0:T(1,128)S(1)}, u32[]{:S(2)}, u32[]{:S(2)}) collective-permute-start(f32[16,1,128]{2,1,0:T(1,128)S(1)} %get-tuple-element.126), channel_id=1, source_target_pairs={{0,4},{4,8},{8,12},{1,5},{5,9},{9,13},{2,6},{6,10},{10,14},{3,7},{... | collective-permute-start | bytes 24584 | tf_op jit(solution)/shard_map/ppermute | solution.py:23
  10.6 13.1 %collective-permute-start.1 = (f32[16,1,128]{2,1,0:T(1,128)S(1)}, f32[16,1,128]{2,1,0:T(1,128)S(1)}, u32[]{:S(2)}, u32[]{:S(2)}) collective-permute-start(f32[16,1,128]{2,1,0:T(1,128)S(1)} %get-tuple-element.125), channel_id=1, source_target_pairs={{4,0},{8,4},{12,8},{5,1},{9,5},{13,9},{6,2},{10,6},{14,10},{7,3},{... | collective-permute-start | bytes 24584 | tf_op jit(solution)/shard_map/ppermute | solution.py:26
  11.9 11.9 %collective-permute-start = (f32[16,1,128]{2,1,0:T(1,128)S(1)}, f32[16,1,128]{2,1,0:T(1,128)S(1)}, u32[]{:S(2)}, u32[]{:S(2)}) collective-permute-start(f32[16,1,128]{2,1,0:T(1,128)S(1)} %get-tuple-element.124), channel_id=1, source_target_pairs={{0,4},{4,8},{8,12},{1,5},{5,9},{9,13},{2,6},{6,10},{10,14},{3,7},{... | collective-permute-start | bytes 24584 | tf_op jit(solution)/shard_map/ppermute | solution.py:23
  17.9 8.5 collective-permute-start.9
  19.2 7.2 collective-permute-start.8
  23.8 8.2 collective-permute-start.2
  25.1 6.9 collective-permute-start.3
  27.6 7.5 collective-permute-start.11
  28.9 6.2 collective-permute-start.10
  54.4 61.3 %collective-permute-start.17 = (f32[18,34,1]{2,1,0:T(8,128)}, f32[18,34,1]{2,1,0:T(8,128)}, u32[]{:S(2)}, u32[]{:S(2)}) collective-permute-start(f32[18,34,1]{2,1,0:T(8,128)} %get-tuple-element.99), channel_id=1, source_target_pairs={{1,0},{3,2},{5,4},{7,6},{9,8},{11,10},{13,12},{15,14},{17,16},{19,... | collective-permute-start | bytes 7352 | tf_op jit(solution)/shard_map/ppermute | solution.py:26
  55.7 60.0 %collective-permute-start.16 = (f32[18,34,1]{2,1,0:T(8,128)}, f32[18,34,1]{2,1,0:T(8,128)}, u32[]{:S(2)}, u32[]{:S(2)}) collective-permute-start(f32[18,34,1]{2,1,0:T(8,128)} %get-tuple-element.98), channel_id=1, source_target_pairs={{0,1},{2,3},{4,5},{6,7},{8,9},{10,11},{12,13},{14,15},{16,17},{18,... | collective-permute-start | bytes 7352 | tf_op jit(solution)/shard_map/ppermute | solution.py:23
  143.7 6.1 collective-permute-start.19
  145.0 6.1 collective-permute-start.18
  151.8 23.1 %collective-permute-start.21 = (f32[1,18,64]{2,0,1:T(1,128)}, f32[1,18,64]{2,0,1:T(1,128)}, u32[]{:S(2)}, u32[]{:S(2)}) collective-permute-start(f32[1,18,64]{2,0,1:T(1,128)} %copy.1398), channel_id=1, source_target_pairs={{2,0},{3,1},{6,4},{7,5},{10,8},{11,9},{14,12},{15,13},{18,16},{19,... | collective-permute-start | bytes 13832 | tf_op jit(solution)/shard_map/ppermute | solution.py:26
  153.6 21.9 %collective-permute-start.20 = (f32[1,18,64]{2,0,1:T(1,128)}, f32[1,18,64]{2,0,1:T(1,128)}, u32[]{:S(2)}, u32[]{:S(2)}) collective-permute-start(f32[1,18,64]{2,0,1:T(1,128)} %copy.1395), channel_id=1, source_target_pairs={{0,2},{1,3},{4,6},{5,7},{8,10},{9,11},{12,14},{13,15},{16,18},{17,... | collective-permute-start | bytes 13832 | tf_op jit(solution)/shard_map/ppermute | solution.py:23
  177.9 18.4 %collective-permute-start.23 = (f32[10,18,1]{2,1,0:T(8,128)}, f32[10,18,1]{2,1,0:T(8,128)}, u32[]{:S(2)}, u32[]{:S(2)}) collective-permute-start(f32[10,18,1]{2,1,0:T(8,128)} %get-tuple-element.147), channel_id=1, source_target_pairs={{1,0},{3,2},{5,4},{7,6},{9,8},{11,10},{13,12},{15,14},{17,16},{19,... | collective-permute-start | bytes 2168 | tf_op jit(solution)/shard_map/ppermute | solution.py:26
  179.2 17.1 %collective-permute-start.22 = (f32[10,18,1]{2,1,0:T(8,128)}, f32[10,18,1]{2,1,0:T(8,128)}, u32[]{:S(2)}, u32[]{:S(2)}) collective-permute-start(f32[10,18,1]{2,1,0:T(8,128)} %get-tuple-element.146), channel_id=1, source_target_pairs={{0,1},{2,3},{4,5},{6,7},{8,9},{10,11},{12,13},{14,15},{16,17},{18,... | collective-permute-start | bytes 2168 | tf_op jit(solution)/shard_map/ppermute | solution.py:23
  201.2 6.1 collective-permute-start.25
  202.5 6.1 collective-permute-start.24
  208.7 8.6 collective-permute-start.27
  210.0 7.3 collective-permute-start.26
  223.1 6.1 collective-permute-start.31
  224.4 6.1 collective-permute-start.30
  242.3 6.1 collective-permute-start.37
  243.6 6.1 collective-permute-start.36
  261.5 6.1 collective-permute-start.43
  262.8 6.1 collective-permute-start.42
  280.7 6.1 collective-permute-start.49
  282.0 6.1 collective-permute-start.48
  299.9 6.1 collective-permute-start.55
  301.2 6.1 collective-permute-start.54
  319.0 6.1 collective-permute-start.61
  338.2 6.1 collective-permute-start.67
  357.6 6.1 collective-permute-start.73
  358.9 6.1 collective-permute-start.72
  377.4 6.1 collective-permute-start.79
  378.7 6.1 collective-permute-start.78
  398.9 6.4 collective-permute-start.85
  400.2 6.2 collective-permute-start.84
  406.4 31.3 %collective-permute-start.87 = (f32[1,34,128]{2,1,0:T(8,128)S(1)}, f32[1,34,128]{2,1,0:T(8,128)S(1)}, u32[]{:S(2)}, u32[]{:S(2)}) collective-permute-start(f32[1,34,128]{2,1,0:T(8,128)S(1)} %get-tuple-element.111), channel_id=1, source_target_pairs={{2,0},{3,1},{6,4},{7,5},{10,8},{11,9},{14,12},{15,13},{18,16},{19,... | collective-permute-start | bytes 52232 | tf_op jit(solution)/shard_map/ppermute | solution.py:26
  407.9 29.8 %collective-permute-start.86 = (f32[1,34,128]{2,1,0:T(8,128)S(1)}, f32[1,34,128]{2,1,0:T(8,128)S(1)}, u32[]{:S(2)}, u32[]{:S(2)}) collective-permute-start(f32[1,34,128]{2,1,0:T(8,128)S(1)} %get-tuple-element.110), channel_id=1, source_target_pairs={{0,2},{1,3},{4,6},{5,7},{8,10},{9,11},{12,14},{13,15},{16,18},{17,... | collective-permute-start | bytes 52232 | tf_op jit(solution)/shard_map/ppermute | solution.py:23
  469.3 6.1 collective-permute-start.91
  470.6 6.3 collective-permute-start.90
  516.1 7.0 collective-permute-start.97
  517.4 6.4 collective-permute-start.96
  524.4 7.0 collective-permute-start.99
  525.7 6.8 collective-permute-start.98
  537.6 10.7 %collective-permute-start.100 = (bf16[16,10,18,1]{2,0,3,1:T(8,128)(2,1)S(1)}, bf16[16,10,18,1]{2,0,3,1:T(8,128)(2,1)}, u32[]{:S(2)}, u32[]{:S(2)}) collective-permute-start(bf16[16,10,18,1]{2,0,3,1:T(8,128)(2,1)S(1)} %copy.1529), channel_id=1, source_target_pairs={{0,1},{2,3},{4,5},{6,7},{8,9},{10,11},{12,13},{14,15},{16,17},{18,... | collective-permute-start | bytes 17288 | tf_op jit(solution)/shard_map/ppermute | solution.py:23
  544.6 10.8 %collective-permute-start.101 = (bf16[16,10,18,1]{2,0,3,1:T(8,128)(2,1)S(1)}, bf16[16,10,18,1]{2,0,3,1:T(8,128)(2,1)}, u32[]{:S(2)}, u32[]{:S(2)}) collective-permute-start(bf16[16,10,18,1]{2,0,3,1:T(8,128)(2,1)S(1)} %copy.1534), channel_id=1, source_target_pairs={{1,0},{3,2},{5,4},{7,6},{9,8},{11,10},{13,12},{15,14},{17,16},{19,... | collective-permute-start | bytes 17288 | tf_op jit(solution)/shard_map/ppermute | solution.py:26
  617.9 6.2 collective-permute-start.103
  619.2 6.4 collective-permute-start.102
  625.7 7.2 collective-permute-start.105
  627.0 7.0 collective-permute-start.104
  675.2 8.7 collective-permute-start.109
  676.5 7.4 collective-permute-start.108
  684.0 6.3 collective-permute-start.111
  685.3 6.4 collective-permute-start.110
  729.8 6.6 collective-permute-start.115
  731.1 6.5 collective-permute-start.114
  738.7 7.7 collective-permute-start.117
  740.0 7.2 collective-permute-start.116
  756.0 17.7 %collective-permute-start.118 = (bf16[32,10,18,1]{0,2,3,1:T(8,128)(2,1)}, bf16[32,10,18,1]{0,2,3,1:T(8,128)(2,1)}, u32[]{:S(2)}, u32[]{:S(2)}) collective-permute-start(bf16[32,10,18,1]{0,2,3,1:T(8,128)(2,1)} %copy.1615), channel_id=1, source_target_pairs={{0,1},{2,3},{4,5},{6,7},{8,9},{10,11},{12,13},{14,15},{16,17},{18,... | collective-permute-start | bytes 34568 | tf_op jit(solution)/shard_map/ppermute | solution.py:23
  765.9 21.5 %collective-permute-start.119 = (bf16[32,10,18,1]{0,2,3,1:T(8,128)(2,1)S(1)}, bf16[32,10,18,1]{0,2,3,1:T(8,128)(2,1)S(1)}, u32[]{:S(2)}, u32[]{:S(2)}) collective-permute-start(bf16[32,10,18,1]{0,2,3,1:T(8,128)(2,1)S(1)} %copy.1619), channel_id=1, source_target_pairs={{1,0},{3,2},{5,4},{7,6},{9,8},{11,10},{13,12},{15,14},{17,16},{19,... | collective-permute-start | bytes 34568 | tf_op jit(solution)/shard_map/ppermute | solution.py:26
  (154 other events, 4351.6 us)
where the time goes:
time: 893 us; the launch traced here: 881 us
  local copies, waits for them, and re-layouts  379 us (42%)
  starting transfers between devices  308 us (34%)
  other arithmetic  112 us (13%)
  waiting for transfers between devices  63.1 us (7%)
  matrix products  14 us (2%)
    ppermute x60, starting transfers between devices, with_halo(): lax.ppermute(lax.slice_in_dim(block, block.shape[dim] - width, None, axis...  230 us
    unnamed x327, local copies, waits for them, and re-layouts  118 us
    reshape x8, local copies, waits for them, and re-layouts, block_sum(): values.reshape(size_x // 2, 2, size_y // 2, 2, size_z // 2, 2)  78.7 us
    ppermute x60, starting transfers between devices, with_halo(): lax.ppermute(lax.slice_in_dim(block, 0, width, axis=dim), axis, backward)  78.4 us
    reshape x5, local copies, waits for them, and re-layouts, conv_valid(): jnp.stack(pieces, axis=1).reshape(in_channels * 27, out_x * out_y * out_z)  70.9 us
    ppermute x60, waiting for transfers between devices, with_halo(): lax.ppermute(lax.slice_in_dim(block, block.shape[dim] - width, None, axis...  44.7 us
    another operation x6, other arithmetic, conv_valid(): jnp.stack(pieces, axis=1).reshape(in_channels * 27, out_x * out_y * out_z)  30.4 us
    reduce_sum x9, other arithmetic, block_sum(): values.reshape(size_x // 2, 2, size_y // 2, 2, size_z // 2, 2)  30.3 us
  transfers between devices with their start and end apart: 120, of which 49 were waited for; matrix products, arithmetic and copies ran while one was open for 19% of the time, Pallas kernels for 0%

commit v1 on v0

v1 whole, which is shorter than its diff:
```python
import functools

import jax
import jax.numpy as jnp
from jax import lax
from jax.experimental import pallas as pl
from jax.experimental.pallas import tpu as pltpu
from jax.sharding import PartitionSpec as P

COARSE_SWEEPS = 8
PERM_TABLE = (0.02, 0.15, 0.8, 2.5, 9.0)
LOG_PERM_TABLE = (-3.912023, -1.89712, -0.223144, 0.916291, 2.197225)
PORE_TABLE = (0.05, 0.12, 0.2, 0.25, 0.3)
storage_factor = 0.0002
vertical_factor = 0.5
relax_weight = 0.6666667
rate_unit = 0.05
MESH = pl.DeviceIdType.MESH
RIM = 3


def table_lookup(facies, table):
    result = jnp.full(facies.shape, table[0], jnp.float32)
    for entry_index in range(1, len(table)):
        result = jnp.where(facies == entry_index, jnp.float32(table[entry_index]), result)
    return result


def harmonic(lower, upper):
    return 2.0 * lower * upper / (lower + upper)


def pair_x(values):
    size_x, size_y, size_z = values.shape
    split = values.reshape(size_x // 2, 2, size_y, size_z)
    return split[:, 0], split[:, 1]


def turn(values, shift, axis):
    return pltpu.roll(values, shift % values.shape[axis], axis)


def even_cells(shape, step, axis):
    index = lax.broadcasted_iota(jnp.int32, shape, axis)
    return (index & step) == 0


def pair_sum(values, step, axis):
    even = even_cells(values.shape, step, axis)
    return values + jnp.where(even, turn(values, -step, axis), turn(values, step, axis))


def take_even(values, step, axis):
    return jnp.where(even_cells(values.shape, step, axis), values, turn(values, step, axis))


def take_odd(values, step, axis):
    return jnp.where(even_cells(values.shape, step, axis), turn(values, -step, axis), values)


def block_sum(values, step):
    low, high = pair_x(values)
    return pair_sum(pair_sum(low + high, step, 1), step, 2)


def with_diagonal(storage, faces):
    diagonal = storage + faces[0] + faces[1] + faces[2] + faces[3] + faces[4] + faces[5]
    return (storage, faces, diagonal)


def coarsen(operator, step):
    storage, faces, _ = operator
    sides_y = [sum(pair_x(faces[i])) for i in (2, 3)]
    sides_z = [sum(pair_x(faces[i])) for i in (4, 5)]
    new_faces = (
        pair_sum(pair_sum(pair_x(faces[0])[0], step, 1), step, 2),
        pair_sum(pair_sum(pair_x(faces[1])[1], step, 1), step, 2),
        take_even(pair_sum(sides_y[0], step, 2), step, 1),
        take_odd(pair_sum(sides_y[1], step, 2), step, 1),
        take_even(pair_sum(sides_z[0], step, 1), step, 2),
        take_odd(pair_sum(sides_z[1], step, 1), step, 2),
    )
    return with_diagonal(block_sum(storage, step), new_faces)


def enlarge_x(values):
    size_x, size_y, size_z = values.shape
    return jnp.broadcast_to(values[:, None], (size_x, 2, size_y, size_z)).reshape(
        size_x * 2, size_y, size_z
    )


def cycle_kernel(sizes, fac_ref, old_ref, col_ref, out_ref, feat_ref, *scratch):
    levels, (send_sem, recv_sem) = scratch[:-2], scratch[-2:]
    levels = [levels[5 * i : 5 * i + 5] for i in range(4)]
    count_x, count_y = sizes
    at_x, at_y, at_z = (lax.axis_index(axis) for axis in ("gx", "gy", "gz"))
    others = (
        (at_x > 0, {"gx": jnp.maximum(at_x - 1, 0)}),
        (at_x < count_x - 1, {"gx": jnp.minimum(at_x + 1, count_x - 1)}),
        (at_y > 0, {"gy": jnp.maximum(at_y - 1, 0)}),
        (at_y < count_y - 1, {"gy": jnp.minimum(at_y + 1, count_y - 1)}),
    )
    partner = {"gz": 1 - at_z}
    for held, outgoing, beside_x, beside_y, beside_z in levels:
        beside_x[...] = jnp.zeros_like(beside_x)
        beside_y[...] = jnp.zeros_like(beside_y)

    barrier = pltpu.get_barrier_semaphore()
    for there, device in others:

        @pl.when(there)
        def _():
            pl.semaphore_signal(barrier, inc=1, device_id=device, device_id_type=MESH)

    pl.semaphore_signal(barrier, inc=1, device_id=partner, device_id_type=MESH)
    peers = 1 + sum(there.astype(jnp.int32) for there, _ in others)
    pl.semaphore_wait(barrier, peers)

    used = [0, 0, 0, 0]
    turn_of = [0]

    def begin(values, level):
        slot = used[level]
        used[level] += 1
        k = turn_of[0]
        turn_of[0] += 1
        held, outgoing, beside_x, beside_y, beside_z = levels[level]
        size_x, size_y, _ = values.shape
        held[slot] = values
        outgoing[slot, 0] = values[:, :1]
        outgoing[slot, 1] = values[:, size_y - 1 :]
        sources = (
            held.at[slot, pl.ds(0, 1)],
            held.at[slot, pl.ds(size_x - 1, 1)],
            outgoing.at[slot, 0],
            outgoing.at[slot, 1],
        )
        targets = (
            beside_x.at[slot, pl.ds(1, 1)],
            beside_x.at[slot, pl.ds(0, 1)],
            beside_y.at[slot, 1],
            beside_y.at[slot, 0],
        )
        copies = []
        for side, (there, device) in enumerate(others):
            back = side ^ 1
            copy = pltpu.make_async_remote_copy(
                sources[side],
                targets[side],
                send_sem.at[k, side],
                recv_sem.at[k, back],
                device_id=device,
                device_id_type=MESH,
            )
            pl.when(there)(copy.start)
            arrival = pltpu.make_async_remote_copy(
                sources[back],
                targets[back],
                send_sem.at[k, side],
                recv_sem.at[k, side],
                device_id=device,
                device_id_type=MESH,
            )
            copies.append((there, copy, arrival))
        across = pltpu.make_async_remote_copy(
            held.at[slot],
            beside_z.at[slot],
            send_sem.at[k, 4],
            recv_sem.at[k, 4],
            device_id=partner,
            device_id_type=MESH,
        )
        across.start()
        return level, slot, copies, across

    def finish(pending):
        level, slot, copies, across = pending
        for there, copy, arrival in copies:

            @pl.when(there)
            def _():
                copy.wait_send()
                arrival.wait_recv()

        across.wait()
        _, _, beside_x, beside_y, beside_z = levels[level]
        return beside_x[slot], beside_y[slot], beside_z[slot]

    def neighbours(values, beside, step):
        along_x, along_y, along_z = beside
        shape = values.shape
        index_y = lax.broadcasted_iota(jnp.int32, shape, 1)
        index_z = lax.broadcasted_iota(jnp.int32, shape, 2)
        size_y, size_z = shape[1:]
        return (
            jnp.concatenate([along_x[:1], values[:-1]], 0),
            jnp.concatenate([values[1:], along_x[1:]], 0),
            jnp.where(index_y < step, along_y[0], turn(values, step, 1)),
            jnp.where(index_y >= size_y - step, along_y[1], turn(values, -step, 1)),
            turn(jnp.where(index_z >= size_z - step, along_z, values), step, 2),
            turn(jnp.where(index_z < step, along_z, values), -step, 2),
        )

    def apply_with(values, beside, operator, step):
        total = operator[2] * values
        for face, other in zip(operator[1], neighbours(values, beside, step)):
            total = total - face * other
        return total

    def apply_level(values, operator, level):
        return apply_with(values, finish(begin(values, level)), operator, 1 << level)

    def relax(values, rhs, operator, level):
        return values + relax_weight * (rhs - apply_level(values, operator, level)) / operator[2]

    facies = fac_ref[...]
    permeability = table_lookup(facies, PERM_TABLE)
    sent_perm = begin(permeability, 0)
    old = old_ref[...]
    sent_old = begin(old, 0)
    storage = storage_factor * table_lookup(facies, PORE_TABLE)
    source = jnp.broadcast_to(rate_unit * col_ref[...], facies.shape)
    rhs = storage * old + source

    around = list(neighbours(permeability, finish(sent_perm), 1))
    index_z = lax.broadcasted_iota(jnp.int32, facies.shape, 2)
    size_z = facies.shape[2]
    around[4] = jnp.where((index_z == 0) & (at_z == 0), 0.0, around[4])
    around[5] = jnp.where((index_z == size_z - 1) & (at_z == 1), 0.0, around[5])
    faces = [harmonic(permeability, other) for other in around]
    faces[4] = vertical_factor * faces[4]
    faces[5] = vertical_factor * faces[5]
    zero = with_diagonal(storage, faces)
    one = coarsen(zero, 1)
    two = coarsen(one, 2)
    three = coarsen(two, 4)

    product = apply_with(old, finish(sent_old), zero, 1)
    state_zero = old + relax_weight * (rhs - product) / zero[2]
    rhs_one = block_sum(rhs - apply_level(state_zero, zero, 0), 1)
    state_one = relax_weight * rhs_one / one[2]
    rhs_two = block_sum(rhs_one - apply_level(state_one, one, 1), 2)
    state_two = relax_weight * rhs_two / two[2]
    rhs_three = block_sum(rhs_two - apply_level(state_two, two, 2), 4)
    state_three = relax_weight * rhs_three / three[2]
    for _ in range(COARSE_SWEEPS - 1):
        state_three = relax(state_three, rhs_three, three, 3)
    state_two = relax(state_two + enlarge_x(state_three), rhs_two, two, 2)
    state_one = relax(state_one + enlarge_x(state_two), rhs_one, one, 1)
    pressure = relax(state_zero + enlarge_x(state_one), rhs, zero, 0)
    out_ref[...] = pressure

    size_x, size_y, _ = facies.shape
    keep_z = (
        lax.broadcasted_iota(jnp.int32, (size_z, size_z // 2), 0)
        == 2 * lax.broadcasted_iota(jnp.int32, (size_z, size_z // 2), 1)
    ).astype(jnp.bfloat16)
    keep_y = (
        2 * lax.broadcasted_iota(jnp.int32, (size_y // 2, size_y), 0)
        == lax.broadcasted_iota(jnp.int32, (size_y // 2, size_y), 1)
    ).astype(jnp.bfloat16)
    for channel, field in enumerate((pressure, table_lookup(facies, LOG_PERM_TABLE), source)):
        mean = (block_sum(field, 1) * 0.125).astype(jnp.bfloat16)
        for plane in range(size_x // 2):
            rows = jnp.dot(keep_y, mean[plane], preferred_element_type=jnp.float32)
            cells = jnp.dot(
                rows.astype(jnp.bfloat16), keep_z, preferred_element_type=jnp.float32
            )
            feat_ref[channel, plane] = cells


def pressure_cycle(facies, pressure_old, column):
    size_x, size_y, size_z = facies.shape
    counts = (4, 2, 2, COARSE_SWEEPS - 1)
    scratch = []
    for level, count in enumerate(counts):
        planes = size_x >> level
        scratch += [
            pltpu.VMEM((count, planes, size_y, size_z), jnp.float32),
            pltpu.VMEM((count, 2, planes, 1, size_z), jnp.float32),
            pltpu.VMEM((count, 2, size_y, size_z), jnp.float32),
            pltpu.VMEM((count, 2, planes, 1, size_z), jnp.float32),
            pltpu.VMEM((count, planes, size_y, size_z), jnp.float32),
        ]
    turns = sum(counts)
    scratch += [pltpu.SemaphoreType.DMA((turns, 5)), pltpu.SemaphoreType.DMA((turns, 5))]
    return pl.pallas_call(
        functools.partial(cycle_kernel, (lax.axis_size("gx"), lax.axis_size("gy"))),
        out_shape=(
            jax.ShapeDtypeStruct(facies.shape, jnp.float32),
            jax.ShapeDtypeStruct((3, size_x // 2, size_y // 2, size_z // 2), jnp.float32),
        ),
        in_specs=[pl.BlockSpec(memory_space=pltpu.VMEM)] * 3,
        out_specs=[pl.BlockSpec(memory_space=pltpu.VMEM)] * 2,
        scratch_shapes=scratch,
        compiler_params=pltpu.CompilerParams(
            collective_id=0, has_side_effects=True, vmem_limit_bytes=48 * 1024 * 1024
        ),
    )(facies, pressure_old, column)


def well_columns(well_x, well_y, well_rate, start_x, start_y, count_x, count_y):
    along_x = (well_x[:, None] == start_x + jnp.arange(count_x, dtype=jnp.int32)[None, :]).astype(
        jnp.float32
    )
    along_y = (well_y[:, None] == start_y + jnp.arange(count_y, dtype=jnp.int32)[None, :]).astype(
        jnp.float32
    )
    weighted = along_x * well_rate.astype(jnp.float32)[:, None]
    return jnp.dot(weighted.T, along_y, precision=lax.Precision.HIGHEST)


def with_halo(block, sides, width):
    for axis, dim in sides:
        count = lax.axis_size(axis)
        forward = [(i, i + 1) for i in range(count - 1)]
        backward = [(target, source) for source, target in forward]
        low = lax.ppermute(
            lax.slice_in_dim(block, block.shape[dim] - width, None, axis=dim), axis, forward
        )
        high = lax.ppermute(lax.slice_in_dim(block, 0, width, axis=dim), axis, backward)
        block = jnp.concatenate([low, block, high], axis=dim)
    return block


def lanes_of(size_y, size_z):
    return -(-((size_y + 2 * RIM) * (size_z + 2 * RIM)) // 128) * 128


def flat_planes(padded):
    channels, size_x, size_y, size_z = padded.shape
    lanes = lanes_of(size_y - 2 * RIM, size_z - 2 * RIM)
    flat = padded.transpose(1, 0, 2, 3).reshape(size_x, channels, size_y * size_z)
    return jnp.pad(flat, ((0, 0), (0, 0), (0, lanes - size_y * size_z)))


def inside_mask(sizes):
    parts = []
    for size, axis in zip(sizes, ("gx", "gy", "gz")):
        index = jnp.arange(size + 2 * RIM) - RIM + lax.axis_index(axis) * size
        parts.append((index >= 0) & (index < size * lax.axis_size(axis)))
    mask = parts[0][:, None, None] & parts[1][None, :, None] & parts[2][None, None, :]
    return flat_planes(mask[None].astype(jnp.float32))


def flat_index(size_y, size_z):
    lanes = lanes_of(size_y, size_z)
    index = jnp.arange(lanes)
    wide = size_z + 2 * RIM
    real = index < wide * (size_y + 2 * RIM)
    return jnp.where(real, index // wide - RIM, -100), jnp.where(real, index % wide - RIM, -100)


def conv_matrix(weight):
    width, channels = weight.shape[:2]
    groups = -(-channels // 16)
    weight = jnp.pad(weight, ((0, 0), (0, groups * 16 - channels), (0, 0), (0, 0), (0, 0)))
    weight = weight.reshape(width, groups, 16, 3, 3, 3).transpose(4, 5, 0, 1, 3, 2)
    return weight.reshape(9 * width, groups * 48)


def conv_plane(matrix, wide, groups):
    stacked = [g.reshape(g.shape[0] * g.shape[1], g.shape[2]) for g in groups]
    stacked = stacked[0] if len(stacked) == 1 else jnp.concatenate(stacked, 0)
    product = jnp.dot(matrix, stacked, preferred_element_type=jnp.float32)
    lanes = product.shape[1]
    total = None
    for shift in range(9):
        offset = (shift // 3 - 1) * wide + shift % 3 - 1
        part = product[16 * shift : 16 * shift + 16]
        if offset:
            part = pltpu.roll(part, (-offset) % lanes, 1)
        total = part if total is None else total + part
    return total


def silu(values):
    return values / (1.0 + jnp.exp(-values))


def encode_kernel(wide, feat_ref, mask_ref, w1_ref, w2_ref, keep_ref, skip_ref, pool_ref, first):
    planes = feat_ref.shape[0]

    @pl.loop(0, planes - 2)
    def _(x):
        values = silu(conv_plane(w1_ref[...], wide, [feat_ref[pl.ds(x, 3)]]))
        first[x] = (jnp.where(mask_ref[x + 1] > 0, values, 0.0)).astype(jnp.bfloat16)

    @pl.loop(0, planes - 4)
    def _(x):
        values = silu(conv_plane(w2_ref[...], wide, [first[pl.ds(x, 3)]]))
        skip_ref[x] = (jnp.where(mask_ref[x + 2] > 0, values, 0.0)).astype(jnp.bfloat16)

    @pl.loop(0, pool_ref.shape[0])
    def _(x):
        total = skip_ref[2 * x + 1].astype(jnp.float32) + skip_ref[2 * x + 2].astype(jnp.float32)
        lanes = total.shape[1]
        total = total + pltpu.roll(total, lanes - 1, 1)
        total = total + pltpu.roll(total, lanes - wide, 1)
        mean = (total * 0.125).astype(jnp.bfloat16)
        pool_ref[x] = jnp.dot(mean, keep_ref[...], preferred_element_type=jnp.float32).astype(
            jnp.bfloat16
        )


def decode_kernel(
    wide, wide_pool, skip_ref, pool_ref, mask_ref, w1_ref, w2_ref, w3_ref, head_ref, up_ref,
    delta_ref, middle, deep, raised,
):
    planes = pool_ref.shape[0]

    @pl.loop(0, planes - 2)
    def _(x):
        values = silu(conv_plane(w1_ref[...], wide_pool, [pool_ref[pl.ds(x, 3)]]))
        middle[x] = (jnp.where(mask_ref[x + 1] > 0, values, 0.0)).astype(jnp.bfloat16)

    @pl.loop(0, planes - 4)
    def _(x):
        values = silu(conv_plane(w2_ref[...], wide_pool, [middle[pl.ds(x, 3)]]))
        values = jnp.where(mask_ref[x + 2] > 0, values, 0.0).astype(jnp.bfloat16)
        deep[x] = jnp.dot(values, up_ref[...], preferred_element_type=jnp.float32).astype(
            jnp.bfloat16
        )

    for x in range(raised.shape[0]):
        raised[x] = deep[(x + 1) // 2]

    @pl.loop(0, delta_ref.shape[0])
    def _(x):
        values = silu(
            conv_plane(w3_ref[...], wide, [skip_ref[pl.ds(x, 3)], raised[pl.ds(x, 3)]])
        )
        values = values.astype(jnp.bfloat16).astype(jnp.float32)
        delta_ref[x] = jnp.sum(values * head_ref[...], axis=0, keepdims=True)


def on_device(
    facies, pressure_old, saturation, well_x, well_y, well_rate,
    enc_first, enc_second, mid_first, mid_second, dec_weight, head_weight,
):
    size_x, size_y, size_z = facies.shape
    column = well_columns(
        well_x, well_y, well_rate,
        lax.axis_index("gx") * size_x, lax.axis_index("gy") * size_y, size_x, size_y,
    )
    pressure, means = pressure_cycle(facies, pressure_old, column[:, :, None])
    blocks = saturation.shape
    pools = tuple(size // 2 for size in blocks)
    sides = (("gy", 2), ("gx", 1), ("gz", 3))
    features = jnp.concatenate([saturation[None], means], 0).astype(jnp.bfloat16)
    features = with_halo(features, sides, RIM)
    features = jnp.pad(features, ((0, 12), (0, 0), (0, 0), (0, 0)))
    planes = flat_planes(features)
    lanes, lanes_pool = lanes_of(*blocks[1:]), lanes_of(*pools[1:])
    wide, wide_pool = blocks[2] + 2 * RIM, pools[2] + 2 * RIM

    row, depth = flat_index(*blocks[1:])
    row_pool, depth_pool = flat_index(*pools[1:])
    own = jnp.arange(pools[1] * pools[2])
    keep = (
        (row[:, None] == 2 * (own // pools[2])[None]) & (depth[:, None] == 2 * (own % pools[2])[None])
    ).astype(jnp.bfloat16)
    raise_matrix = (
        (row_pool[:, None] == jnp.floor_divide(row, 2)[None])
        & (depth_pool[:, None] == jnp.floor_divide(depth, 2)[None])
        & (row_pool > -100)[:, None]
    ).astype(jnp.bfloat16)

    whole = pl.BlockSpec(memory_space=pltpu.VMEM)
    limit = pltpu.CompilerParams(vmem_limit_bytes=48 * 1024 * 1024)
    skip, pooled = pl.pallas_call(
        functools.partial(encode_kernel, wide),
        out_shape=(
            jax.ShapeDtypeStruct((blocks[0] + 2, 16, lanes), jnp.bfloat16),
            jax.ShapeDtypeStruct((pools[0], 16, pools[1] * pools[2]), jnp.bfloat16),
        ),
        in_specs=[whole] * 5,
        out_specs=[whole] * 2,
        scratch_shapes=[pltpu.VMEM((blocks[0] + 4, 16, lanes), jnp.bfloat16)],
        compiler_params=limit,
    )(planes, inside_mask(blocks), conv_matrix(enc_first), conv_matrix(enc_second), keep)
    pooled = pooled.transpose(1, 0, 2).reshape(16, *pools)
    pooled = flat_planes(with_halo(pooled, sides, RIM))
    delta = pl.pallas_call(
        functools.partial(decode_kernel, wide, wide_pool),
        out_shape=jax.ShapeDtypeStruct((blocks[0], 1, lanes), jnp.float32),
        in_specs=[whole] * 8,
        out_specs=whole,
        scratch_shapes=[
            pltpu.VMEM((pools[0] + 4, 16, lanes_pool), jnp.bfloat16),
            pltpu.VMEM((pools[0] + 2, 16, lanes), jnp.bfloat16),
            pltpu.VMEM((blocks[0] + 2, 16, lanes), jnp.bfloat16),
        ],
        compiler_params=limit,
    )(
        skip, pooled, inside_mask(pools), conv_matrix(mid_first), conv_matrix(mid_second),
        conv_matrix(dec_weight), head_weight.astype(jnp.float32)[:, None], raise_matrix,
    )
    delta = delta[:, 0, : wide * (blocks[1] + 2 * RIM)]
    delta = delta.reshape(blocks[0], blocks[1] + 2 * RIM, wide)
    delta = delta[:, RIM : RIM + blocks[1], RIM : RIM + blocks[2]]
    return (pressure, saturation + delta)


def solution(mesh):
    return jax.shard_map(
        on_device,
        mesh=mesh,
        in_specs=(P(("run", "gx"), "gy", "gz"),) * 3 + (P("run"),) * 3 + (P(),) * 6,
        out_specs=(P(("run", "gx"), "gy", "gz"), P(("run", "gx"), "gy", "gz")),
        check_vma=False,
    )
```

time: 893 us -> 161 us (0.18); the launches traced: 881 us -> 160 us
  local copies, waits for them, and re-layouts: 379 us -> 34.1 us
  starting transfers between devices: 308 us -> 33.9 us
  other arithmetic: 112 us -> 10.5 us
  Pallas kernels: 0 us -> 70.4 us
  waiting for transfers between devices: 63.1 us -> 8.74 us
  matrix products: 14 us -> 0.93 us
    ppermute x60 -> x6, starting transfers between devices: 230 us -> 26.1 us  [with_halo(): lax.ppermute(lax.slice_in_dim(block, block.shape[dim] - width, None, axis...]
    reshape x33 -> x15, local copies, waits for them, and re-layouts: 162 us -> 10.3 us  [the longest x3 5.68 us: flat_planes(): padded.transpose(1, 0, 2, 3).reshape(size_x, channels, size_y * size_z)]
    unnamed x327 -> x47, local copies, waits for them, and re-layouts: 118 us -> 10.5 us
    ppermute x60 -> x6, starting transfers between devices: 78.4 us -> 7.72 us  [with_halo(): lax.ppermute(lax.slice_in_dim(block, 0, width, axis=dim), axis, backward)]
    pallas_call x0 -> x3, Pallas kernels: none -> 70.4 us  [the longest x1 48.9 us: pressure_cycle(): pl.pallas_call(functools.partial(cycle_kernel, (lax.axis_size('gx'), lax....]
    reduce_sum x28 -> x0, other arithmetic: 48 us -> none  [the longest x9 30.3 us: block_sum(): values.reshape(size_x // 2, 2, size_y // 2, 2, size_z // 2, 2)]
    ppermute x60 -> x6, waiting for transfers between devices: 44.7 us -> 2.83 us  [with_halo(): lax.ppermute(lax.slice_in_dim(block, block.shape[dim] - width, None, axis...]
    another operation x8 -> x1, other arithmetic: 30.5 us -> 0.02 us  [the longest x6 30.4 us: conv_valid(): jnp.stack(pieces, axis=1).reshape(in_channels * 27, out_x * out_y * out_z)]
  transfers between devices with their start and end apart: 120 -> 12, of which waited for: 49 -> 5; matrix products, arithmetic and copies ran while one was open for 19% -> 10% of each run, Pallas kernels for 0% -> 0%
where the time goes in v1:
time: 161 us; the launch traced here: 160 us
  Pallas kernels  70.4 us (44%)
  local copies, waits for them, and re-layouts  34.1 us (21%)
  starting transfers between devices  33.9 us (21%)
  other arithmetic  10.5 us (7%)
  waiting for transfers between devices  8.74 us (5%)
    pallas_call x1, Pallas kernels, pressure_cycle(): pl.pallas_call(functools.partial(cycle_kernel, (lax.axis_size('gx'), lax....  48.9 us
    ppermute x6, starting transfers between devices, with_halo(): lax.ppermute(lax.slice_in_dim(block, block.shape[dim] - width, None, axis...  26.1 us
    pallas_call x1, Pallas kernels, on_device(): pl.pallas_call(functools.partial(encode_kernel, wide), out_shape=(jax.Sha...  11.1 us
    unnamed x47, local copies, waits for them, and re-layouts  10.5 us
    pallas_call x1, Pallas kernels, on_device(): pl.pallas_call(functools.partial(decode_kernel, wide, wide_pool), out_sha...  10.4 us
    ppermute x6, starting transfers between devices, with_halo(): lax.ppermute(lax.slice_in_dim(block, 0, width, axis=dim), axis, backward)  7.72 us
    ppermute x6, waiting for transfers between devices, with_halo(): lax.ppermute(lax.slice_in_dim(block, 0, width, axis=dim), axis, backward)  5.91 us
    reshape x3, local copies, waits for them, and re-layouts, flat_planes(): padded.transpose(1, 0, 2, 3).reshape(size_x, channels, size_y * size_z)  5.68 us
  transfers between devices with their start and end apart: 12, of which 5 were waited for; matrix products, arithmetic and copies ran while one was open for 10% of the time, Pallas kernels for 0%

profile of v1, /device:TPU:0, one launch (start us, length us, event | category | flops | bytes accessed | tf_op | source)
XLA Modules:
  0.0 159.9 jit_solution(15796914794584640933)
XLA Ops:
  0.7 0.7 convert_element_type.45
  1.4 0.9 convolution_bitcast_fusion
  2.3 0.2 copy.53.col_ref
  2.5 0.9 copy-done.1
  3.4 0.9 copy-done.2
  4.4 48.9 %shard_map.131 = (f32[16,32,128]{2,1,0:T(8,128)S(1)}, f32[3,8,16,64]{3,2,1,0:T(8,128)S(1)}) custom-call(s32[16,32,128]{2,1,0:T(8,128)S(1)} %copy-done.1, f32[16,32,128]{2,1,0:T(8,128)S(1)} %copy-done.2, f32[16,32,1]{2,1,0:T(8,128)S(1)} %copy.53.col_ref), custom_call_target="tpu_custom_call" | custom-call | tf_op jit(solution)/shard_map/pallas_call | solution.py:288
  53.3 0.7 copy-done.3
  54.1 1.3 collective-permute-start.1
  55.4 4.5 %collective-permute-start = (bf16[4,8,3,64]{3,2,1,0:T(4,128)(2,1)S(1)}, bf16[4,8,3,64]{3,2,1,0:T(4,128)(2,1)S(1)}, u32[]{:S(2)}, u32[]{:S(2)}) collective-permute-start(bf16[4,8,3,64]{3,2,1,0:T(4,128)(2,1)S(1)} %get-tuple-element.20), channel_id=1, source_target_pairs={{0,4},{4,8},{8,12},{1,5},{5,9},{9,13},{2,6},{6,10},{10,14},{3,7},{... | collective-permute-start | bytes 36872 | tf_op jit(solution)/shard_map/ppermute | solution.py:319
  60.3 0.2 and.281
  60.7 0.7 pad_convert_fusion.mask_ref
  61.5 1.1 and_convert_fusion.1.keep_ref
  62.5 1.2 and_convert_fusion.up_ref
  63.9 0.7 pad_maximum_fusion.6
  64.6 1.3 collective-permute-start.3
  65.9 4.5 %collective-permute-start.2 = (bf16[4,3,22,64]{3,2,1,0:T(8,128)(2,1)S(1)}, bf16[4,3,22,64]{3,2,1,0:T(8,128)(2,1)S(1)}, u32[]{:S(2)}, u32[]{:S(2)}) collective-permute-start(bf16[4,3,22,64]{3,2,1,0:T(8,128)(2,1)S(1)} %get-tuple-element.16), channel_id=1, source_target_pairs={{0,2},{1,3},{4,6},{5,7},{8,10},{9,11},{12,14},{13,15},{16,18},{17,... | collective-permute-start | bytes 101384 | tf_op jit(solution)/shard_map/ppermute | solution.py:319
  70.5 0.6 collective-permute-done.3
  71.0 1.4 collective-permute-done.2
  72.4 0.1 pad_maximum_fusion.1
  72.5 1.0 fusion.41
  73.6 1.3 collective-permute-start.5
  74.9 4.5 %collective-permute-start.4 = (bf16[4,14,22,3]{3,2,1,0:T(8,128)(2,1)}, bf16[4,14,22,3]{3,2,1,0:T(8,128)(2,1)}, u32[]{:S(2)}, u32[]{:S(2)}) collective-permute-start(bf16[4,14,22,3]{3,2,1,0:T(8,128)(2,1)} %get-tuple-element.12), channel_id=1, source_target_pairs={{0,1},{2,3},{4,5},{6,7},{8,9},{10,11},{12,13},{14,15},{16,17},{18,... | collective-permute-start | bytes 22184 | tf_op jit(solution)/shard_map/ppermute | solution.py:319
  79.4 0.1 copy.76
  79.5 0.1 reshape.393.w1_ref
  79.7 1.0 copy.77
  80.6 0.7 reshape.394.w2_ref
  81.5 0.7 and.282
  82.3 1.6 %pad_maximum_fusion.2 = bf16[4,14,22,70]{3,2,1,0:T(8,128)(2,1)S(1)} fusion(bf16[4,14,22,3]{3,2,1,0:T(8,128)(2,1)} %collective-permute-done.5, bf16[4,3,22,64]{3,2,1,0:T(8,128)(2,1)} %copy-done.11, bf16[4,8,3,64]{3,2,1,0:T(4,128)(2,1)S(1)} %collective-permute-done.1, bf16[3,8,16,64]{3,2,1,0:T(8,128)(2,1)S(1)} %convert.13, ...), kind=kLoop, calls=%fused_computation.8 | loop fusion | flops 1379840 | bytes 344960 | tf_op jit(solution)/shard_map/concatenate | solution.py:323
  83.9 1.3 pad_bitcast_fusion
  85.2 3.1 %reshape.392 = bf16[14,16,1540]{2,0,1:T(8,128)(2,1)} reshape(bf16[14,16,22,70]{3,2,0,1:T(8,128)(2,1)} %pad_bitcast_fusion) | data formatting | bytes 1379840 | tf_op jit(solution)/shard_map/reshape | solution.py:334
  88.3 1.3 copy.75
  89.7 11.1 %shard_map.132 = (bf16[10,16,1664]{2,1,0:T(8,128)(2,1)S(1)}, bf16[4,16,256]{2,1,0:T(8,128)(2,1)S(1)}) custom-call(bf16[14,16,1664]{2,1,0:T(8,128)(2,1)S(1)} %pad.29.feat_ref, f32[14,1,1664]{2,1,0:T(1,128)S(1)} %copy-done, bf16[144,48]{1,0:T(8,128)(2,1)S(1)} %reshape.393.w1_ref, bf16[144,48]{1,0:T(8,128)(2,1)S(1)} %copy-done.5, ...), custom_call_target="tpu_custom_call" | custom-call | tf_op jit(solution)/shard_map/pallas_call | solution.py:472
  100.9 0.6 copy-done.6
  101.5 0.9 reshape.383
  102.5 3.5 %collective-permute-start.6 = (bf16[16,4,3,32]{3,0,2,1:T(8,128)(2,1)S(1)}, bf16[16,4,3,32]{3,0,2,1:T(8,128)(2,1)S(1)}, u32[]{:S(2)}, u32[]{:S(2)}) collective-permute-start(bf16[16,4,3,32]{3,0,2,1:T(8,128)(2,1)S(1)} %copy.88), channel_id=1, source_target_pairs={{0,4},{4,8},{8,12},{1,5},{5,9},{9,13},{2,6},{6,10},{10,14},{3,7},{... | collective-permute-start | bytes 36872 | tf_op jit(solution)/shard_map/ppermute | solution.py:319
  106.0 0.8 broadcast_and_fusion.1
  106.8 1.3 collective-permute-start.7
  108.2 4.6 %collective-permute-done.7 = bf16[16,4,3,32]{3,0,2,1:T(8,128)(2,1)S(1)} collective-permute-done((bf16[16,4,3,32]{3,0,2,1:T(8,128)(2,1)S(1)}, bf16[16,4,3,32]{3,0,2,1:T(8,128)(2,1)S(1)}, u32[]{:S(2)}, u32[]{:S(2)}) %collective-permute-start.7) | collective-permute-done | bytes 12320 | tf_op jit(solution)/shard_map/ppermute | solution.py:322
  112.8 1.3 collective-permute-start.9
  114.1 4.7 %collective-permute-start.8 = (bf16[16,3,14,32]{3,0,2,1:T(8,128)(2,1)S(1)}, bf16[16,3,14,32]{3,0,2,1:T(8,128)(2,1)S(1)}, u32[]{:S(2)}, u32[]{:S(2)}) collective-permute-start(bf16[16,3,14,32]{3,0,2,1:T(8,128)(2,1)S(1)} %get-tuple-element.14), channel_id=1, source_target_pairs={{0,2},{1,3},{4,6},{5,7},{8,10},{9,11},{12,14},{13,15},{16,18},{17,... | collective-permute-start | bytes 129032 | tf_op jit(solution)/shard_map/ppermute | solution.py:319
  118.9 0.5 bitcast_convert_fusion
  119.4 0.7 collective-permute-done.9
  120.1 1.5 collective-permute-done.8
  121.6 0.7 copy-done.9
  122.3 0.1 pad_maximum_fusion
  122.4 1.3 fusion.40
  123.7 2.9 %copy.85 = bf16[16,10,14,3]{2,0,3,1:T(8,128)(2,1)} copy(bf16[16,10,14,3]{3,0,2,1:T(8,128)(2,1)} %get-tuple-element.11) | data formatting | bytes 26880
  126.6 1.3 collective-permute-start.11
  127.9 2.9 %copy.84 = bf16[16,10,14,3]{2,0,3,1:T(8,128)(2,1)} copy(bf16[16,10,14,3]{3,0,2,1:T(8,128)(2,1)} %get-tuple-element.10) | data formatting | bytes 26880
  130.7 4.3 %collective-permute-start.10 = (bf16[16,10,14,3]{2,0,3,1:T(8,128)(2,1)}, bf16[16,10,14,3]{2,0,3,1:T(8,128)(2,1)}, u32[]{:S(2)}, u32[]{:S(2)}) collective-permute-start(bf16[16,10,14,3]{2,0,3,1:T(8,128)(2,1)} %copy.84), channel_id=1, source_target_pairs={{0,1},{2,3},{4,5},{6,7},{8,9},{10,11},{12,13},{14,15},{16,17},{18,... | collective-permute-start | bytes 40328 | tf_op jit(solution)/shard_map/ppermute | solution.py:319
  135.5 1.0 reshape.389
  136.5 0.2 copy.90
  136.8 0.2 reshape.390.w3_ref
  136.9 0.8 copy.74.head_ref
  137.7 2.9 %copy.66 = bf16[16,10,14,3]{3,0,2,1:T(8,128)(2,1)} copy(bf16[16,10,14,3]{2,0,3,1:T(8,128)(2,1)} %collective-permute-done.11) | data formatting | bytes 26880 | tf_op jit(solution)/shard_map/ppermute | solution.py:322
  140.6 3.0 %copy.65 = bf16[16,10,14,3]{3,0,2,1:T(8,128)(2,1)} copy(bf16[16,10,14,3]{2,0,3,1:T(8,128)(2,1)} %collective-permute-done.10) | data formatting | bytes 26880 | tf_op jit(solution)/shard_map/ppermute | solution.py:319
  143.6 1.8 %maximum_bitcast_fusion = bf16[10,16,14,38]{3,1,2,0:T(8,128)(2,1)S(1)} fusion(bf16[16,10,14,3]{3,0,2,1:T(8,128)(2,1)} %copy.66, bf16[16,3,14,32]{3,0,2,1:T(8,128)(2,1)S(1)} %copy-done.8, bf16[16,4,14,32]{3,0,2,1:T(8,128)(2,1)S(1)} %constant_dynamic-update-slice_fusion, bf16[16,3,14,32]{3,0,2,1:T(8,128)(2,1)S(1)} %copy-done.10, bf16[16,10,14,3]{3,0,2,1:T(8,128)(2,1)} %copy.65), kind=kLoop, calls=%fused_computation.5 | loop fusion | flops 851200 | bytes 340480 | tf_op jit(solution)/shard_map/transpose | solution.py:334
  145.4 0.2 copy.67
  145.6 1.3 reshape.384
  146.8 1.0 pad.33.pool_ref
  147.8 10.4 %shard_map.133 = f32[8,1,1664]{2,1,0:T(1,128)S(1)} custom-call(bf16[10,16,1664]{2,1,0:T(8,128)(2,1)S(1)} %get-tuple-element.8.skip_ref, bf16[10,16,640]{2,1,0:T(8,128)(2,1)S(1)} %pad.33.pool_ref, f32[10,1,640]{2,1,0:T(1,128)S(1)} %pad_convert_fusion.1.mask_ref, bf16[144,48]{1,0:T(8,128)(2,1)S(1)} %reshape.395.w1_ref, bf16[144,48]{1,0:T(8,128)(2,1)S(1)} %reshape.396.w2_ref, ...), custom_call_target="tpu_custom_call" | custom-call | tf_op jit(solution)/shard_map/pallas_call | solution.py:485
  158.2 0.1 slice_reduce_fusion
  158.5 0.7 slice_add_fusion
  159.2 0.7 copy.94
  (82 shorter events, 1.7 us)
Async XLA Ops:
  0.6 53.4 %copy-start.14 = (f32[8,16,64]{2,1,0:T(8,128)S(1)}, f32[8,16,64]{2,1,0:T(8,128)}, u32[]{:S(2)}) copy-start(f32[8,16,64]{2,1,0:T(8,128)} %param.14) | copy-start | bytes 98308
  2.5 1.0 copy-start.1
  3.4 0.9 copy-start.2
  53.3 0.7 copy-start.3
  54.1 9.8 %collective-permute-start.1 = (bf16[4,8,3,64]{3,2,1,0:T(4,128)(2,1)S(1)}, bf16[4,8,3,64]{3,2,1,0:T(4,128)(2,1)S(1)}, u32[]{:S(2)}, u32[]{:S(2)}) collective-permute-start(bf16[4,8,3,64]{3,2,1,0:T(4,128)(2,1)S(1)} %get-tuple-element.21), channel_id=1, source_target_pairs={{4,0},{8,4},{12,8},{5,1},{9,5},{13,9},{6,2},{10,6},{14,10},{7,3},{... | collective-permute-start | bytes 36872 | tf_op jit(solution)/shard_map/ppermute | solution.py:322
  55.4 8.5 %collective-permute-start = (bf16[4,8,3,64]{3,2,1,0:T(4,128)(2,1)S(1)}, bf16[4,8,3,64]{3,2,1,0:T(4,128)(2,1)S(1)}, u32[]{:S(2)}, u32[]{:S(2)}) collective-permute-start(bf16[4,8,3,64]{3,2,1,0:T(4,128)(2,1)S(1)} %get-tuple-element.20), channel_id=1, source_target_pairs={{0,4},{4,8},{8,12},{1,5},{5,9},{9,13},{2,6},{6,10},{10,14},{3,7},{... | collective-permute-start | bytes 36872 | tf_op jit(solution)/shard_map/ppermute | solution.py:319
  62.5 7.9 %copy-start.18 = (bf16[16,4,3,3,3]{0,1,4,3,2:T(4,128)(2,1)S(1)}, bf16[16,4,3,3,3]{0,1,4,3,2:T(4,128)(2,1)}, u32[]{:S(2)}) copy-start(bf16[16,4,3,3,3]{0,1,4,3,2:T(4,128)(2,1)} %param.18) | copy-start | bytes 10372
  63.9 9.7 %copy-start.13 = (bf16[4,8,3,64]{3,2,1,0:T(4,128)(2,1)}, bf16[4,8,3,64]{3,2,1,0:T(4,128)(2,1)S(1)}, u32[]{:S(2)}) copy-start(bf16[4,8,3,64]{3,2,1,0:T(4,128)(2,1)S(1)} %collective-permute-done) | copy-start | bytes 36868
  64.6 6.4 %collective-permute-start.3 = (bf16[4,3,22,64]{3,2,1,0:T(8,128)(2,1)}, bf16[4,3,22,64]{3,2,1,0:T(8,128)(2,1)S(1)}, u32[]{:S(2)}, u32[]{:S(2)}) collective-permute-start(bf16[4,3,22,64]{3,2,1,0:T(8,128)(2,1)} %get-tuple-element.17), channel_id=1, source_target_pairs={{2,0},{3,1},{6,4},{7,5},{10,8},{11,9},{14,12},{15,13},{18,16},{19,... | collective-permute-start | bytes 101384 | tf_op jit(solution)/shard_map/ppermute | solution.py:322
  65.9 6.5 %collective-permute-start.2 = (bf16[4,3,22,64]{3,2,1,0:T(8,128)(2,1)S(1)}, bf16[4,3,22,64]{3,2,1,0:T(8,128)(2,1)S(1)}, u32[]{:S(2)}, u32[]{:S(2)}) collective-permute-start(bf16[4,3,22,64]{3,2,1,0:T(8,128)(2,1)S(1)} %get-tuple-element.16), channel_id=1, source_target_pairs={{0,2},{1,3},{4,6},{5,7},{8,10},{9,11},{12,14},{13,15},{16,18},{17,... | collective-permute-start | bytes 101384 | tf_op jit(solution)/shard_map/ppermute | solution.py:319
  71.0 8.5 %copy-start.11 = (bf16[4,3,22,64]{3,2,1,0:T(8,128)(2,1)}, bf16[4,3,22,64]{3,2,1,0:T(8,128)(2,1)S(1)}, u32[]{:S(2)}) copy-start(bf16[4,3,22,64]{3,2,1,0:T(8,128)(2,1)S(1)} %collective-permute-done.3) | copy-start | bytes 101380
  72.4 7.0 %copy-start.12 = (bf16[4,3,22,64]{3,2,1,0:T(8,128)(2,1)}, bf16[4,3,22,64]{3,2,1,0:T(8,128)(2,1)S(1)}, u32[]{:S(2)}) copy-start(bf16[4,3,22,64]{3,2,1,0:T(8,128)(2,1)S(1)} %collective-permute-done.2) | copy-start | bytes 101380
  73.6 8.7 %collective-permute-start.5 = (bf16[4,14,22,3]{3,2,1,0:T(8,128)(2,1)}, bf16[4,14,22,3]{3,2,1,0:T(8,128)(2,1)}, u32[]{:S(2)}, u32[]{:S(2)}) collective-permute-start(bf16[4,14,22,3]{3,2,1,0:T(8,128)(2,1)} %get-tuple-element.13), channel_id=1, source_target_pairs={{1,0},{3,2},{5,4},{7,6},{9,8},{11,10},{13,12},{15,14},{17,16},{19,... | collective-permute-start | bytes 22184 | tf_op jit(solution)/shard_map/ppermute | solution.py:322
  74.9 7.4 %collective-permute-start.4 = (bf16[4,14,22,3]{3,2,1,0:T(8,128)(2,1)}, bf16[4,14,22,3]{3,2,1,0:T(8,128)(2,1)}, u32[]{:S(2)}, u32[]{:S(2)}) collective-permute-start(bf16[4,14,22,3]{3,2,1,0:T(8,128)(2,1)} %get-tuple-element.12), channel_id=1, source_target_pairs={{0,1},{2,3},{4,5},{6,7},{8,9},{10,11},{12,13},{14,15},{16,17},{18,... | collective-permute-start | bytes 22184 | tf_op jit(solution)/shard_map/ppermute | solution.py:319
  88.3 1.4 copy-start
  88.3 1.4 copy-start.5
  100.9 0.6 copy-start.6
  101.5 17.4 %copy-start.19 = (bf16[16]{0:T(256)(128)(2,1)S(1)}, bf16[16]{0:T(256)(128)(2,1)}, u32[]{:S(2)}) copy-start(bf16[16]{0:T(256)(128)(2,1)} %param.23) | copy-start | bytes 100
  102.5 5.6 %collective-permute-start.6 = (bf16[16,4,3,32]{3,0,2,1:T(8,128)(2,1)S(1)}, bf16[16,4,3,32]{3,0,2,1:T(8,128)(2,1)S(1)}, u32[]{:S(2)}, u32[]{:S(2)}) collective-permute-start(bf16[16,4,3,32]{3,0,2,1:T(8,128)(2,1)S(1)} %copy.88), channel_id=1, source_target_pairs={{0,4},{4,8},{8,12},{1,5},{5,9},{9,13},{2,6},{6,10},{10,14},{3,7},{... | collective-permute-start | bytes 36872 | tf_op jit(solution)/shard_map/ppermute | solution.py:319
  106.8 6.0 %collective-permute-start.7 = (bf16[16,4,3,32]{3,0,2,1:T(8,128)(2,1)S(1)}, bf16[16,4,3,32]{3,0,2,1:T(8,128)(2,1)S(1)}, u32[]{:S(2)}, u32[]{:S(2)}) collective-permute-start(bf16[16,4,3,32]{3,0,2,1:T(8,128)(2,1)S(1)} %copy.89), channel_id=1, source_target_pairs={{4,0},{8,4},{12,8},{5,1},{9,5},{13,9},{6,2},{10,6},{14,10},{7,3},{... | collective-permute-start | bytes 36872 | tf_op jit(solution)/shard_map/ppermute | solution.py:322
  112.8 7.3 %collective-permute-start.9 = (bf16[16,3,14,32]{3,0,2,1:T(8,128)(2,1)S(1)}, bf16[16,3,14,32]{3,0,2,1:T(8,128)(2,1)S(1)}, u32[]{:S(2)}, u32[]{:S(2)}) collective-permute-start(bf16[16,3,14,32]{3,0,2,1:T(8,128)(2,1)S(1)} %get-tuple-element.15), channel_id=1, source_target_pairs={{2,0},{3,1},{6,4},{7,5},{10,8},{11,9},{14,12},{15,13},{18,16},{19,... | collective-permute-start | bytes 129032 | tf_op jit(solution)/shard_map/ppermute | solution.py:322
  114.1 7.5 %collective-permute-start.8 = (bf16[16,3,14,32]{3,0,2,1:T(8,128)(2,1)S(1)}, bf16[16,3,14,32]{3,0,2,1:T(8,128)(2,1)S(1)}, u32[]{:S(2)}, u32[]{:S(2)}) collective-permute-start(bf16[16,3,14,32]{3,0,2,1:T(8,128)(2,1)S(1)} %get-tuple-element.14), channel_id=1, source_target_pairs={{0,2},{1,3},{4,6},{5,7},{8,10},{9,11},{12,14},{13,15},{16,18},{17,... | collective-permute-start | bytes 129032 | tf_op jit(solution)/shard_map/ppermute | solution.py:319
  120.1 1.5 copy-start.7
  121.6 0.7 copy-start.9
  123.7 11.4 %copy-start.16 = (bf16[16,16,3,3,3]{1,0,4,3,2:T(8,128)(2,1)S(1)}, bf16[16,16,3,3,3]{1,0,4,3,2:T(8,128)(2,1)}, u32[]{:S(2)}) copy-start(bf16[16,16,3,3,3]{1,0,4,3,2:T(8,128)(2,1)} %param.20) | copy-start | bytes 41476
  123.7 11.6 %copy-start.17 = (bf16[16,16,3,3,3]{1,0,4,3,2:T(8,128)(2,1)S(1)}, bf16[16,16,3,3,3]{1,0,4,3,2:T(8,128)(2,1)}, u32[]{:S(2)}) copy-start(bf16[16,16,3,3,3]{1,0,4,3,2:T(8,128)(2,1)} %param.21) | copy-start | bytes 41476
  126.6 11.1 %collective-permute-start.11 = (bf16[16,10,14,3]{2,0,3,1:T(8,128)(2,1)}, bf16[16,10,14,3]{2,0,3,1:T(8,128)(2,1)}, u32[]{:S(2)}, u32[]{:S(2)}) collective-permute-start(bf16[16,10,14,3]{2,0,3,1:T(8,128)(2,1)} %copy.85), channel_id=1, source_target_pairs={{1,0},{3,2},{5,4},{7,6},{9,8},{11,10},{13,12},{15,14},{17,16},{19,... | collective-permute-start | bytes 40328 | tf_op jit(solution)/shard_map/ppermute | solution.py:322
  130.7 9.9 %collective-permute-start.10 = (bf16[16,10,14,3]{2,0,3,1:T(8,128)(2,1)}, bf16[16,10,14,3]{2,0,3,1:T(8,128)(2,1)}, u32[]{:S(2)}, u32[]{:S(2)}) collective-permute-start(bf16[16,10,14,3]{2,0,3,1:T(8,128)(2,1)} %copy.84), channel_id=1, source_target_pairs={{0,1},{2,3},{4,5},{6,7},{8,9},{10,11},{12,13},{14,15},{16,17},{18,... | collective-permute-start | bytes 40328 | tf_op jit(solution)/shard_map/ppermute | solution.py:319
  136.7 6.9 %copy-start.8 = (bf16[16,3,14,32]{3,0,2,1:T(8,128)(2,1)S(1)}, bf16[16,3,14,32]{3,0,2,1:T(8,128)(2,1)}, u32[]{:S(2)}) copy-start(bf16[16,3,14,32]{3,0,2,1:T(8,128)(2,1)} %copy-done.7) | copy-start | bytes 129028
  136.9 6.7 %copy-start.10 = (bf16[16,3,14,32]{3,0,2,1:T(8,128)(2,1)S(1)}, bf16[16,3,14,32]{3,0,2,1:T(8,128)(2,1)}, u32[]{:S(2)}) copy-start(bf16[16,3,14,32]{3,0,2,1:T(8,128)(2,1)} %copy-done.9) | copy-start | bytes 129028
  147.8 10.7 %copy-start.15 = (f32[8,16,64]{2,1,0:T(8,128)S(1)}, f32[8,16,64]{2,1,0:T(8,128)}, u32[]{:S(2)}) copy-start(f32[8,16,64]{2,1,0:T(8,128)} %param.14) | copy-start | bytes 98308
  147.8 11.4 %copy-start.4 = (f32[16,32,128]{2,1,0:T(8,128)S(1)}, f32[16,32,128]{2,1,0:T(8,128)}, u32[]{:S(2)}) copy-start(f32[16,32,128]{2,1,0:T(8,128)} %copy-done.3) | copy-start | bytes 786436

commit v2 on v1

--- a/solution.py
+++ b/solution.py
@@ -2,6 +2,8 @@
 
 import jax
 import jax.numpy as jnp
+import ml_dtypes
+import numpy as np
 from jax import lax
 from jax.experimental import pallas as pl
 from jax.experimental.pallas import tpu as pltpu
@@ -311,128 +313,279 @@
     return jnp.dot(weighted.T, along_y, precision=lax.Precision.HIGHEST)
 
 
-def with_halo(block, sides, width):
-    for axis, dim in sides:
-        count = lax.axis_size(axis)
-        forward = [(i, i + 1) for i in range(count - 1)]
-        backward = [(target, source) for source, target in forward]
-        low = lax.ppermute(
-            lax.slice_in_dim(block, block.shape[dim] - width, None, axis=dim), axis, forward
-        )
-        high = lax.ppermute(lax.slice_in_dim(block, 0, width, axis=dim), axis, backward)
-        block = jnp.concatenate([low, block, high], axis=dim)
-    return block
-
-
 def lanes_of(size_y, size_z):
     return -(-((size_y + 2 * RIM) * (size_z + 2 * RIM)) // 128) * 128
 
 
-def flat_planes(padded):
-    channels, size_x, size_y, size_z = padded.shape
-    lanes = lanes_of(size_y - 2 * RIM, size_z - 2 * RIM)
-    flat = padded.transpose(1, 0, 2, 3).reshape(size_x, channels, size_y * size_z)
-    return jnp.pad(flat, ((0, 0), (0, 0), (0, lanes - size_y * size_z)))
-
-
-def inside_mask(sizes):
-    parts = []
-    for size, axis in zip(sizes, ("gx", "gy", "gz")):
-        index = jnp.arange(size + 2 * RIM) - RIM + lax.axis_index(axis) * size
-        parts.append((index >= 0) & (index < size * lax.axis_size(axis)))
-    mask = parts[0][:, None, None] & parts[1][None, :, None] & parts[2][None, None, :]
-    return flat_planes(mask[None].astype(jnp.float32))
-
-
 def flat_index(size_y, size_z):
-    lanes = lanes_of(size_y, size_z)
-    index = jnp.arange(lanes)
+    index = np.arange(lanes_of(size_y, size_z))
     wide = size_z + 2 * RIM
     real = index < wide * (size_y + 2 * RIM)
-    return jnp.where(real, index // wide - RIM, -100), jnp.where(real, index % wide - RIM, -100)
-
-
-def conv_matrix(weight):
-    width, channels = weight.shape[:2]
-    groups = -(-channels // 16)
-    weight = jnp.pad(weight, ((0, 0), (0, groups * 16 - channels), (0, 0), (0, 0), (0, 0)))
-    weight = weight.reshape(width, groups, 16, 3, 3, 3).transpose(4, 5, 0, 1, 3, 2)
-    return weight.reshape(9 * width, groups * 48)
-
-
-def conv_plane(matrix, wide, groups):
-    stacked = [g.reshape(g.shape[0] * g.shape[1], g.shape[2]) for g in groups]
-    stacked = stacked[0] if len(stacked) == 1 else jnp.concatenate(stacked, 0)
-    product = jnp.dot(matrix, stacked, preferred_element_type=jnp.float32)
-    lanes = product.shape[1]
-    total = None
-    for shift in range(9):
-        offset = (shift // 3 - 1) * wide + shift % 3 - 1
-        part = product[16 * shift : 16 * shift + 16]
-        if offset:
-            part = pltpu.roll(part, (-offset) % lanes, 1)
-        total = part if total is None else total + part
-    return total
+    row = np.where(real, index // wide - RIM, -100)
+    depth = np.where(real, index % wide - RIM, -100)
+    return row.astype(np.int32), depth.astype(np.int32)
+
+
+def own_planes(values):
+    channels, size_x, size_y, size_z = values.shape
+    lanes = lanes_of(size_y, size_z)
+    wide = size_z + 2 * RIM
+    padded = jnp.pad(values, ((0, 16 - channels), (0, 0), (0, 0), (0, 2 * RIM)))
+    flat = padded.transpose(1, 0, 2, 3).reshape(size_x, 16, size_y * wide)
+    start = RIM * wide + RIM
+    return jnp.pad(flat, ((0, 0), (0, 0), (start, lanes - start - size_y * wide)))
+
+
+def conv_matrices(*weights):
+    groups = []
+    for weight in weights:
+        channels = weight.shape[1]
+        if channels < 16:
+            weight = jnp.pad(weight, ((0, 0), (0, 16 - channels), (0, 0), (0, 0), (0, 0)))
+        groups += [weight[:, at : at + 16] for at in range(0, weight.shape[1], 16)]
+    stacked = jnp.stack(groups).reshape(len(groups), 16, 16, 3, 9)
+    return stacked.transpose(0, 4, 1, 3, 2).reshape(len(groups), 144, 48)
 
 
 def silu(values):
     return values / (1.0 + jnp.exp(-values))
 
 
-def encode_kernel(wide, feat_ref, mask_ref, w1_ref, w2_ref, keep_ref, skip_ref, pool_ref, first):
-    planes = feat_ref.shape[0]
-
-    @pl.loop(0, planes - 2)
+def network_kernel(
+    sizes, blocks, feat_ref, weight_ref, index_ref, pool_index_ref, keep_ref, up_ref, head_ref,
+    delta_ref, fields, first, skip, pooled, middle, deep, raised,
+    own, own_pool, far, far_pool, rows_in, rows_in_pool, rows_out, rows_out_pool,
+    send_sem, recv_sem,
+):
+    count_x, count_y = sizes
+    at_x, at_y, at_z = (lax.axis_index(axis) for axis in ("gx", "gy", "gz"))
+    lower = {"gx": jnp.maximum(at_x - 1, 0)}, {"gy": jnp.maximum(at_y - 1, 0)}
+    upper = (
+        {"gx": jnp.minimum(at_x + 1, count_x - 1)},
+        {"gy": jnp.minimum(at_y + 1, count_y - 1)},
+    )
+    has = ((at_x > 0, at_x < count_x - 1), (at_y > 0, at_y < count_y - 1))
+    partner = {"gz": 1 - at_z}
+    for ref in (fields, pooled, rows_in, rows_in_pool):
+        ref[...] = jnp.zeros_like(ref)
+
+    barrier = pltpu.get_barrier_semaphore()
+    for axis in range(2):
+        for there, device in ((has[axis][0], lower[axis]), (has[axis][1], upper[axis])):
+
+            @pl.when(there)
+            def _():
+                pl.semaphore_signal(barrier, inc=1, device_id=device, device_id_type=MESH)
+
+    pl.semaphore_signal(barrier, inc=1, device_id=partner, device_id_type=MESH)
+    peers = 1 + sum(there.astype(jnp.int32) for pair in has for there in pair)
+    pl.semaphore_wait(barrier, peers)
+
+    def swap(k, axis, to_low, from_low, to_high, from_high):
+        low = pltpu.make_async_remote_copy(
+            to_low, from_high, send_sem.at[k, 0], recv_sem.at[k, 1],
+            device_id=lower[axis], device_id_type=MESH,
+        )
+        high = pltpu.make_async_remote_copy(
+            to_high, from_low, send_sem.at[k, 1], recv_sem.at[k, 0],
+            device_id=upper[axis], device_id_type=MESH,
+        )
+        pl.when(has[axis][0])(low.start)
+        pl.when(has[axis][1])(high.start)
+
+        @pl.when(has[axis][0])
+        def _():
+            low.wait_send()
+            high.wait_recv()
+
+        @pl.when(has[axis][1])
+        def _():
+            high.wait_send()
+            low.wait_recv()
+
+    def fill_rims(k, mine, beyond, sent, landed, whole, row, depth, size_y, size_z):
+        lanes = mine.shape[2]
+        wide = size_z + 2 * RIM
+        across = pltpu.make_async_remote_copy(
+            mine, beyond, send_sem.at[k, 0], recv_sem.at[k, 0],
+            device_id=partner, device_id_type=MESH,
+        )
+        across.start()
+        across.wait()
+        planes = mine.shape[0]
+        here = (row >= 0) & (row < size_y)
+        from_high = here & (depth >= size_z) & (at_z == 0)
+        from_low = here & (depth < 0) & (at_z == 1)
+        low_at, low_len = low_lanes(size_y, size_z)
+        high_at, high_len = high_lanes(size_y, size_z)
+        for x in range(planes):
+            other = beyond[x].astype(jnp.float32)
+            values = mine[x].astype(jnp.float32)
+            values = jnp.where(from_high, pltpu.roll(other, size_z, 1), values)
+            values = jnp.where(from_low, pltpu.roll(other, lanes - size_z, 1), values)
+            values = values.astype(jnp.bfloat16)
+            whole[x + RIM] = values
+            sent[0, x, :, :low_len] = values[:, low_at : low_at + low_len]
+            sent[1, x, :, :high_len] = values[:, high_at : high_at + high_len]
+        swap(k + 1, 1, sent.at[0], landed.at[0], sent.at[1], landed.at[1])
+        for x in range(planes):
+            values = whole[x + RIM].astype(jnp.float32)
+            above = jnp.concatenate(
+                [landed[0, x].astype(jnp.float32), jnp.zeros((16, lanes - landed.shape[3]), jnp.float32)], 1
+            )
+            below = jnp.concatenate(
+                [landed[1, x].astype(jnp.float32), jnp.zeros((16, lanes - landed.shape[3]), jnp.float32)], 1
+            )
+            above = pltpu.roll(above, (high_at - size_y * wide) % lanes, 1)
+            below = pltpu.roll(below, (low_at + size_y * wide) % lanes, 1)
+            values = jnp.where((row < 0) & (row >= -RIM), above, values)
+            values = jnp.where(row >= size_y, below, values)
+            whole[x + RIM] = values.astype(jnp.bfloat16)
+        swap(
+            k + 2, 0,
+            whole.at[pl.ds(RIM, RIM)], whole.at[pl.ds(0, RIM)],
+            whole.at[pl.ds(planes, RIM)], whole.at[pl.ds(planes + RIM, RIM)],
+        )
+
+    def on_grid(row, depth, size_y, size_z):
+        row, depth = row + at_y * size_y, depth + at_z * size_z
+        return (row >= 0) & (row < size_y * count_y) & (depth >= 0) & (depth < 2 * size_z)
+
+    def conv(wide, pieces):
+        product = None
+        for group, planes in pieces:
+            stacked = planes.reshape(48, planes.shape[2])
+            term = jnp.dot(weight_ref[group], stacked, preferred_element_type=jnp.float32)
+            product = term if product is None else product + term
+        lanes = product.shape[1]
+        total = None
+        for shift in range(9):
+            offset = (shift // 3 - 1) * wide + shift % 3 - 1
+            part = product[16 * shift : 16 * shift + 16]
+            if offset:
+                part = pltpu.roll(part, (-offset) % lanes, 1)
+            total = part if total is None else total + part
+        return silu(total)
+
+    size_x, size_y, size_z = blocks
+    pool_x, pool_y, pool_z = (size // 2 for size in blocks)
+    wide, wide_pool = size_z + 2 * RIM, pool_z + 2 * RIM
+    row, depth = index_ref[0:1], index_ref[1:2]
+    row_pool, depth_pool = pool_index_ref[0:1], pool_index_ref[1:2]
+    grid = on_grid(row, depth, size_y, size_z)
+    grid_pool = on_grid(row_pool, depth_pool, pool_y, pool_z)
+
+    def masked(values, mask, plane, size):
+        plane = plane + at_x * size
+        inside = jnp.where((plane >= 0) & (plane < size * count_x), 1.0, 0.0)
+        return (jnp.where(mask, values, 0.0) * inside).astype(jnp.bfloat16)
+
+    own[...] = feat_ref[...]
+    fill_rims(0, own, far, rows_out, rows_in, fields, row, depth, size_y, size_z)
+
+    @pl.loop(0, size_x + 4)
     def _(x):
-        values = silu(conv_plane(w1_ref[...], wide, [feat_ref[pl.ds(x, 3)]]))
-        first[x] = (jnp.where(mask_ref[x + 1] > 0, values, 0.0)).astype(jnp.bfloat16)
-
-    @pl.loop(0, planes - 4)
+        first[x] = masked(conv(wide, [(0, fields[pl.ds(x, 3)])]), grid, x - 2, size_x)
+
+    @pl.loop(0, size_x + 2)
     def _(x):
-        values = silu(conv_plane(w2_ref[...], wide, [first[pl.ds(x, 3)]]))
-        skip_ref[x] = (jnp.where(mask_ref[x + 2] > 0, values, 0.0)).astype(jnp.bfloat16)
-
-    @pl.loop(0, pool_ref.shape[0])
+        skip[x] = masked(conv(wide, [(1, first[pl.ds(x, 3)])]), grid, x - 1, size_x)
+
+    @pl.loop(0, pool_x)
     def _(x):
-        total = skip_ref[2 * x + 1].astype(jnp.float32) + skip_ref[2 * x + 2].astype(jnp.float32)
+        total = skip[2 * x + 1].astype(jnp.float32) + skip[2 * x + 2].astype(jnp.float32)
         lanes = total.shape[1]
         total = total + pltpu.roll(total, lanes - 1, 1)
         total = total + pltpu.roll(total, lanes - wide, 1)
         mean = (total * 0.125).astype(jnp.bfloat16)
-        pool_ref[x] = jnp.dot(mean, keep_ref[...], preferred_element_type=jnp.float32).astype(
+        own_pool[x] = jnp.dot(mean, keep_ref[...], preferred_element_type=jnp.float32).astype(
             jnp.bfloat16
         )
 
-
-def decode_kernel(
-    wide, wide_pool, skip_ref, pool_ref, mask_ref, w1_ref, w2_ref, w3_ref, head_ref, up_ref,
-    delta_ref, middle, deep, raised,
-):
-    planes = pool_ref.shape[0]
-
-    @pl.loop(0, planes - 2)
+    fill_rims(
+        3, own_pool, far_pool, rows_out_pool, rows_in_pool, pooled, row_pool, depth_pool,
+        pool_y, pool_z,
+    )
+
+    @pl.loop(0, pool_x + 4)
     def _(x):
-        values = silu(conv_plane(w1_ref[...], wide_pool, [pool_ref[pl.ds(x, 3)]]))
-        middle[x] = (jnp.where(mask_ref[x + 1] > 0, values, 0.0)).astype(jnp.bfloat16)
-
-    @pl.loop(0, planes - 4)
+        middle[x] = masked(conv(wide_pool, [(2, pooled[pl.ds(x, 3)])]), grid_pool, x - 2, pool_x)
+
+    @pl.loop(0, pool_x + 2)
     def _(x):
-        values = silu(conv_plane(w2_ref[...], wide_pool, [middle[pl.ds(x, 3)]]))
-        values = jnp.where(mask_ref[x + 2] > 0, values, 0.0).astype(jnp.bfloat16)
+        values = masked(conv(wide_pool, [(3, middle[pl.ds(x, 3)])]), grid_pool, x - 1, pool_x)
         deep[x] = jnp.dot(values, up_ref[...], preferred_element_type=jnp.float32).astype(
             jnp.bfloat16
         )
 
-    for x in range(raised.shape[0]):
+    for x in range(size_x + 2):
         raised[x] = deep[(x + 1) // 2]
 
-    @pl.loop(0, delta_ref.shape[0])
+    @pl.loop(0, size_x)
     def _(x):
-        values = silu(
-            conv_plane(w3_ref[...], wide, [skip_ref[pl.ds(x, 3)], raised[pl.ds(x, 3)]])
-        )
+        values = conv(wide, [(4, skip[pl.ds(x, 3)]), (5, raised[pl.ds(x, 3)])])
         values = values.astype(jnp.bfloat16).astype(jnp.float32)
         delta_ref[x] = jnp.sum(values * head_ref[...], axis=0, keepdims=True)
+
+
+def low_lanes(size_y, size_z):
+    wide = size_z + 2 * RIM
+    start = RIM * wide // 128 * 128
+    return start, -(-(2 * RIM * wide) // 128) * 128 - start
+
+
+def high_lanes(size_y, size_z):
+    wide = size_z + 2 * RIM
+    start = size_y * wide // 128 * 128
+    return start, -(-((size_y + RIM) * wide) // 128) * 128 - start
+
+
+def network(features, weights, head, blocks):
+    pools = tuple(size // 2 for size in blocks)
+    lanes, lanes_pool = lanes_of(*blocks[1:]), lanes_of(*pools[1:])
+    edge, edge_pool = (
+        max(low_lanes(*s[1:])[1], high_lanes(*s[1:])[1]) for s in (blocks, pools)
+    )
+    row, depth = flat_index(*blocks[1:])
+    row_pool, depth_pool = flat_index(*pools[1:])
+    owned = (row_pool >= 0) & (row_pool < pools[1]) & (depth_pool >= 0) & (depth_pool < pools[2])
+    keep = (row[:, None] == 2 * row_pool[None]) & (depth[:, None] == 2 * depth_pool[None])
+    keep = (keep & owned[None]).astype(ml_dtypes.bfloat16)
+    up = (row_pool[:, None] == (row // 2)[None]) & (depth_pool[:, None] == (depth // 2)[None])
+    up = (up & (row_pool > -100)[:, None]).astype(ml_dtypes.bfloat16)
+    whole = pl.BlockSpec(memory_space=pltpu.VMEM)
+    x, px, half = blocks[0], pools[0], jnp.bfloat16
+    return pl.pallas_call(
+        functools.partial(network_kernel, (lax.axis_size("gx"), lax.axis_size("gy")), blocks),
+        out_shape=jax.ShapeDtypeStruct((x, 1, lanes), jnp.float32),
+        in_specs=[whole] * 7,
+        out_specs=whole,
+        scratch_shapes=[
+            pltpu.VMEM((x + 2 * RIM, 16, lanes), half),
+            pltpu.VMEM((x + 4, 16, lanes), half),
+            pltpu.VMEM((x + 2, 16, lanes), half),
+            pltpu.VMEM((px + 2 * RIM, 16, lanes_pool), half),
+            pltpu.VMEM((px + 4, 16, lanes_pool), half),
+            pltpu.VMEM((px + 2, 16, lanes), half),
+            pltpu.VMEM((x + 2, 16, lanes), half),
+            pltpu.VMEM((x, 16, lanes), half),
+            pltpu.VMEM((px, 16, lanes_pool), half),
+            pltpu.VMEM((x, 16, lanes), half),
+            pltpu.VMEM((px, 16, lanes_pool), half),
+            pltpu.VMEM((2, x, 16, edge), half),
+            pltpu.VMEM((2, px, 16, edge_pool), half),
+            pltpu.VMEM((2, x, 16, edge), half),
+            pltpu.VMEM((2, px, 16, edge_pool), half),
+            pltpu.SemaphoreType.DMA((6, 2)),
+            pltpu.SemaphoreType.DMA((6, 2)),
+        ],
+        compiler_params=pltpu.CompilerParams(
+            collective_id=1, has_side_effects=True, vmem_limit_bytes=48 * 1024 * 1024
+        ),
+    )(
+        features, weights, jnp.asarray(np.stack([row, depth])),
+        jnp.asarray(np.stack([row_pool, depth_pool])), jnp.asarray(keep), jnp.asarray(up), head,
+    )
 
 
 def on_device(
@@ -446,60 +599,14 @@
     )
     pressure, means = pressure_cycle(facies, pressure_old, column[:, :, None])
     blocks = saturation.shape
-    pools = tuple(size // 2 for size in blocks)
-    sides = (("gy", 2), ("gx", 1), ("gz", 3))
+    wide = blocks[2] + 2 * RIM
     features = jnp.concatenate([saturation[None], means], 0).astype(jnp.bfloat16)
-    features = with_halo(features, sides, RIM)
-    features = jnp.pad(features, ((0, 12), (0, 0), (0, 0), (0, 0)))
-    planes = flat_planes(features)
-    lanes, lanes_pool = lanes_of(*blocks[1:]), lanes_of(*pools[1:])
-    wide, wide_pool = blocks[2] + 2 * RIM, pools[2] + 2 * RIM
-
-    row, depth = flat_index(*blocks[1:])
-    row_pool, depth_pool = flat_index(*pools[1:])
-    own = jnp.arange(pools[1] * pools[2])
-    keep = (
-        (row[:, None] == 2 * (own // pools[2])[None]) & (depth[:, None] == 2 * (own % pools[2])[None])
-    ).astype(jnp.bfloat16)
-    raise_matrix = (
-        (row_pool[:, None] == jnp.floor_divide(row, 2)[None])
-        & (depth_pool[:, None] == jnp.floor_divide(depth, 2)[None])
-        & (row_pool > -100)[:, None]
-    ).astype(jnp.bfloat16)
-
-    whole = pl.BlockSpec(memory_space=pltpu.VMEM)
-    limit = pltpu.CompilerParams(vmem_limit_bytes=48 * 1024 * 1024)
-    skip, pooled = pl.pallas_call(
-        functools.partial(encode_kernel, wide),
-        out_shape=(
-            jax.ShapeDtypeStruct((blocks[0] + 2, 16, lanes), jnp.bfloat16),
-            jax.ShapeDtypeStruct((pools[0], 16, pools[1] * pools[2]), jnp.bfloat16),
-        ),
-        in_specs=[whole] * 5,
-        out_specs=[whole] * 2,
-        scratch_shapes=[pltpu.VMEM((blocks[0] + 4, 16, lanes), jnp.bfloat16)],
-        compiler_params=limit,
-    )(planes, inside_mask(blocks), conv_matrix(enc_first), conv_matrix(enc_second), keep)
-    pooled = pooled.transpose(1, 0, 2).reshape(16, *pools)
-    pooled = flat_planes(with_halo(pooled, sides, RIM))
-    delta = pl.pallas_call(
-        functools.partial(decode_kernel, wide, wide_pool),
-        out_shape=jax.ShapeDtypeStruct((blocks[0], 1, lanes), jnp.float32),
-        in_specs=[whole] * 8,
-        out_specs=whole,
-        scratch_shapes=[
-            pltpu.VMEM((pools[0] + 4, 16, lanes_pool), jnp.bfloat16),
-            pltpu.VMEM((pools[0] + 2, 16, lanes), jnp.bfloat16),
-            pltpu.VMEM((blocks[0] + 2, 16, lanes), jnp.bfloat16),
-        ],
-        compiler_params=limit,
-    )(
-        skip, pooled, inside_mask(pools), conv_matrix(mid_first), conv_matrix(mid_second),
-        conv_matrix(dec_weight), head_weight.astype(jnp.float32)[:, None], raise_matrix,
-    )
-    delta = delta[:, 0, : wide * (blocks[1] + 2 * RIM)]
-    delta = delta.reshape(blocks[0], blocks[1] + 2 * RIM, wide)
-    delta = delta[:, RIM : RIM + blocks[1], RIM : RIM + blocks[2]]
+    weights = conv_matrices(enc_first, enc_second, mid_first, mid_second, dec_weight)
+    delta = network(
+        own_planes(features), weights, head_weight.astype(jnp.float32)[:, None], blocks
+    )
+    delta = delta[:, 0, RIM * wide + RIM : RIM * wide + RIM + blocks[1] * wide]
+    delta = delta.reshape(blocks[0], blocks[1], wide)[:, :, : blocks[2]]
     return (pressure, saturation + delta)
 
 

time: 161 us -> 106 us (0.66)
  starting transfers between devices: 33.9 us -> 0 us
  local copies, waits for them, and re-layouts: 34.1 us -> 8.7 us
  Pallas kernels: 70.4 us -> 92.6 us
  waiting for transfers between devices: 8.74 us -> 0 us
  other arithmetic: 10.5 us -> 2.35 us
    ppermute x12 -> x0, starting transfers between devices: 33.9 us -> none  [the longest x6 26.1 us: with_halo(): lax.ppermute(lax.slice_in_dim(block, block.shape[dim] - width, None, axis...]
    pallas_call x2 -> x1, Pallas kernels: 21.5 us -> 43.7 us  [network(): pl.pallas_call(functools.partial(network_kernel, (lax.axis_size('gx'), la...]
    ppermute x12 -> x0, waiting for transfers between devices: 8.74 us -> none  [the longest x6 5.91 us: with_halo(): lax.ppermute(lax.slice_in_dim(block, 0, width, axis=dim), axis, backward)]
    reshape x15 -> x3, local copies, waits for them, and re-layouts: 10.3 us -> 2.18 us  [the longest x1 1.61 us: conv_matrices(): return stacked.transpose(0, 4, 1, 3, 2).reshape(len(groups), 144, 48)]
    ppermute x2 -> x0, local copies, waits for them, and re-layouts: 5.88 us -> none  [the longest x1 2.96 us: with_halo(): lax.ppermute(lax.slice_in_dim(block, block.shape[dim] - width, None, axis...]
    unnamed x47 -> x34, local copies, waits for them, and re-layouts: 10.5 us -> 5.52 us
    convert_element_type x2 -> x0, other arithmetic: 2.29 us -> none  [the longest x1 1.24 us: on_device(): raise_matrix = ((row_pool[:, None] == jnp.floor_divide(row, 2)[None]) & (...]
    slice x5 -> x2, local copies, waits for them, and re-layouts: 2.52 us -> 0.25 us  [the longest x1 0.15 us: on_device(): delta = delta[:, 0, RIM * wide + RIM:RIM * wide + RIM + blocks[1] * wide]]
  transfers between devices with their start and end apart: 12 -> 0, of which waited for: 5 -> 0; matrix products, arithmetic and copies ran while one was open for 10% -> 0% of each run, Pallas kernels for 0% -> 0%
where the time goes in v2:
time: 106 us; the launch traced here: 105 us
  Pallas kernels  92.6 us (87%)
  local copies, waits for them, and re-layouts  8.7 us (8%)
  other arithmetic  2.35 us (2%)
    pallas_call x1, Pallas kernels, pressure_cycle(): pl.pallas_call(functools.partial(cycle_kernel, (lax.axis_size('gx'), lax....  48.9 us
    pallas_call x1, Pallas kernels, network(): pl.pallas_call(functools.partial(network_kernel, (lax.axis_size('gx'), la...  43.7 us
    unnamed x34, local copies, waits for them, and re-layouts  5.52 us

profile of v2, /device:TPU:0, one launch (start us, length us, event | category | flops | bytes accessed | tf_op | source)
XLA Modules:
  0.0 105.5 jit_solution(18160128018493949098)
XLA Ops:
  0.6 0.7 convert_element_type.6
  1.3 0.9 convolution_bitcast_fusion
  2.2 0.0 copy-start.12
  2.2 0.2 copy.26.col_ref
  2.4 0.0 copy-start.2
  2.4 0.9 copy-done.2
  3.4 0.0 copy-start.3
  3.4 0.9 copy-done.3
  4.3 48.9 %shard_map.167 = (f32[16,32,128]{2,1,0:T(8,128)S(1)}, f32[3,8,16,64]{3,2,1,0:T(8,128)S(1)}) custom-call(s32[16,32,128]{2,1,0:T(8,128)S(1)} %copy-done.2, f32[16,32,128]{2,1,0:T(8,128)S(1)} %copy-done.3, f32[16,32,1]{2,1,0:T(8,128)S(1)} %copy.26.col_ref), custom_call_target="tpu_custom_call" | custom-call | tf_op jit(solution)/shard_map/pallas_call | solution.py:290
  53.3 0.0 copy-start.9
  53.3 0.0 copy-start.10
  53.3 0.0 copy-start.11
  53.3 0.9 convert_bitcast_fusion
  54.2 0.0 copy-start.7
  54.2 0.1 fusion.6
  54.4 0.5 reshape.39
  54.9 0.0 copy-start.13
  54.9 0.0 copy-start
  55.0 0.0 copy-start.4
  55.0 0.0 copy-start.5
  55.0 0.2 pad.13.feat_ref
  55.1 0.0 copy-done.12
  55.2 0.1 copy.28
  55.3 0.1 constant_dynamic-update-slice_fusion
  55.4 0.0 copy-done.9
  55.4 0.1 copy_dynamic-update-slice_fusion.4
  55.5 0.0 copy-done.10
  55.5 0.1 copy_dynamic-update-slice_fusion.3
  55.6 0.0 copy-done.11
  55.6 0.1 copy_dynamic-update-slice_fusion.2
  55.7 0.0 copy-done.7
  55.7 0.1 fusion.17
  55.8 0.1 copy_dynamic-update-slice_fusion.1
  55.9 0.1 copy_dynamic-update-slice_fusion
  56.0 0.0 copy-start.6
  56.0 0.9 copy-done.6
  56.9 1.6 %reshape.37.weight_ref = bf16[6,144,48]{2,1,0:T(8,128)(2,1)S(1)} reshape(bf16[6,9,16,3,16]{4,3,2,1,0:T(4,128)(2,1)} %bitcast.20) | data formatting | bytes 165888 | tf_op jit(solution)/shard_map/reshape | solution.py:347
  58.5 0.0 copy-done.13
  58.5 0.1 copy.34.head_ref
  58.6 0.0 copy-done
  58.6 0.0 copy-done.4
  58.6 0.0 copy-done.5
  58.6 0.0 copy-start.1
  58.6 1.6 %copy-done.1 = bf16[640,1664]{1,0:T(8,128)(2,1)S(1)} copy-done((bf16[640,1664]{1,0:T(8,128)(2,1)S(1)}, bf16[640,1664]{1,0:T(8,128)(2,1)}, u32[]{:S(2)}) %copy-start.1) | copy-done | bytes 2129944
  60.2 0.0 copy-start.8
  60.2 43.7 %shard_map.168 = f32[8,1,1664]{2,1,0:T(1,128)S(1)} custom-call(bf16[8,16,1664]{2,1,0:T(8,128)(2,1)S(1)} %pad.13.feat_ref, bf16[6,144,48]{2,1,0:T(8,128)(2,1)S(1)} %reshape.37.weight_ref, s32[2,1664]{1,0:T(2,128)S(1)} %copy-done.4, s32[2,640]{1,0:T(2,128)S(1)} %copy-done.5, bf16[1664,640]{1,0:T(8,128)(2,1)S(1)} %copy-done, bf16[640,1664]{1,0:T(8,128)(2,1)S(1)} %copy-done.1, ...), custom_call_target="tpu_custom_call" | custom-call | tf_op jit(solution)/shard_map/pallas_call | solution.py:558
  103.9 0.2 slice_reduce_fusion
  104.0 0.1 reshape_squeeze.3
  104.1 0.0 copy-done.8
  104.1 0.6 slice_add_fusion
  104.8 0.7 copy.47
  (6 shorter events, 0.1 us)
Async XLA Ops:
  2.2 52.9 %copy-start.12 = (bf16[16,4,3,3,3]{0,1,4,3,2:T(4,128)(2,1)S(1)}, bf16[16,4,3,3,3]{0,1,4,3,2:T(4,128)(2,1)}, u32[]{:S(2)}) copy-start(bf16[16,4,3,3,3]{0,1,4,3,2:T(4,128)(2,1)} %param.22) | copy-start | bytes 10372
  2.4 1.0 copy-start.2
  3.4 0.9 copy-start.3
  53.3 2.1 %copy-start.9 = (bf16[16,16,3,3,3]{1,0,4,3,2:T(8,128)(2,1)S(1)}, bf16[16,16,3,3,3]{1,0,4,3,2:T(8,128)(2,1)}, u32[]{:S(2)}) copy-start(bf16[16,16,3,3,3]{1,0,4,3,2:T(8,128)(2,1)} %param.23) | copy-start | bytes 41476
  53.3 2.2 %copy-start.10 = (bf16[16,16,3,3,3]{1,0,4,3,2:T(8,128)(2,1)S(1)}, bf16[16,16,3,3,3]{1,0,4,3,2:T(8,128)(2,1)}, u32[]{:S(2)}) copy-start(bf16[16,16,3,3,3]{1,0,4,3,2:T(8,128)(2,1)} %param.24) | copy-start | bytes 41476
  53.3 2.3 %copy-start.11 = (bf16[16,16,3,3,3]{1,0,4,3,2:T(8,128)(2,1)S(1)}, bf16[16,16,3,3,3]{1,0,4,3,2:T(8,128)(2,1)}, u32[]{:S(2)}) copy-start(bf16[16,16,3,3,3]{1,0,4,3,2:T(8,128)(2,1)} %param.25) | copy-start | bytes 41476
  54.2 1.4 %copy-start.7 = (bf16[16,32,3,3,3]{1,0,4,3,2:T(8,128)(2,1)S(1)}, bf16[16,32,3,3,3]{1,0,4,3,2:T(8,128)(2,1)}, u32[]{:S(2)}) copy-start(bf16[16,32,3,3,3]{1,0,4,3,2:T(8,128)(2,1)} %param.26) | copy-start | bytes 82948
  54.9 3.6 %copy-start.13 = (bf16[16]{0:T(256)(128)(2,1)S(1)}, bf16[16]{0:T(256)(128)(2,1)}, u32[]{:S(2)}) copy-start(bf16[16]{0:T(256)(128)(2,1)} %param.27) | copy-start | bytes 100
  54.9 3.7 %copy-start = (bf16[1664,640]{1,0:T(8,128)(2,1)S(1)}, bf16[1664,640]{1,0:T(8,128)(2,1)}, u32[]{:S(2)}) copy-start(bf16[1664,640]{1,0:T(8,128)(2,1)} %constant.28.clone.keep_ref) | copy-start | bytes 6389764
  55.0 3.6 %copy-start.4 = (s32[2,1664]{1,0:T(2,128)S(1)}, s32[2,1664]{1,0:T(2,128)}, u32[]{:S(2)}) copy-start(s32[2,1664]{1,0:T(2,128)} %constant.26.clone.index_ref) | copy-start | bytes 39940
  55.0 3.6 %copy-start.5 = (s32[2,640]{1,0:T(2,128)S(1)}, s32[2,640]{1,0:T(2,128)}, u32[]{:S(2)}) copy-start(s32[2,640]{1,0:T(2,128)} %constant.27.clone.pool_index_ref) | copy-start | bytes 15364
  56.0 0.9 copy-start.6
  58.6 1.6 %copy-start.1 = (bf16[640,1664]{1,0:T(8,128)(2,1)S(1)}, bf16[640,1664]{1,0:T(8,128)(2,1)}, u32[]{:S(2)}) copy-start(bf16[640,1664]{1,0:T(8,128)(2,1)} %constant.29.clone.up_ref) | copy-start | bytes 6389764
  60.2 43.9 %copy-start.8 = (f32[8,16,64]{2,1,0:T(8,128)S(1)}, f32[8,16,64]{2,1,0:T(8,128)}, u32[]{:S(2)}) copy-start(f32[8,16,64]{2,1,0:T(8,128)} %param.18) | copy-start | bytes 98308

commit v3 on v2

--- a/solution.py
+++ b/solution.py
@@ -234,24 +234,26 @@
     faces[4] = vertical_factor * faces[4]
     faces[5] = vertical_factor * faces[5]
     zero = with_diagonal(storage, faces)
+    product = apply_with(old, finish(sent_old), zero, 1)
+    state_zero = old + relax_weight * (rhs - product) / zero[2]
+    sent_zero = begin(state_zero, 0)
     one = coarsen(zero, 1)
     two = coarsen(one, 2)
     three = coarsen(two, 4)
-
-    product = apply_with(old, finish(sent_old), zero, 1)
-    state_zero = old + relax_weight * (rhs - product) / zero[2]
-    rhs_one = block_sum(rhs - apply_level(state_zero, zero, 0), 1)
+    scale_three = relax_weight / three[2]
+    rhs_one = block_sum(rhs - apply_with(state_zero, finish(sent_zero), zero, 1), 1)
     state_one = relax_weight * rhs_one / one[2]
     rhs_two = block_sum(rhs_one - apply_level(state_one, one, 1), 2)
     state_two = relax_weight * rhs_two / two[2]
     rhs_three = block_sum(rhs_two - apply_level(state_two, two, 2), 4)
     state_three = relax_weight * rhs_three / three[2]
     for _ in range(COARSE_SWEEPS - 1):
-        state_three = relax(state_three, rhs_three, three, 3)
+        product = apply_level(state_three, three, 3)
+        state_three = state_three + scale_three * (rhs_three - product)
     state_two = relax(state_two + enlarge_x(state_three), rhs_two, two, 2)
     state_one = relax(state_one + enlarge_x(state_two), rhs_one, one, 1)
-    pressure = relax(state_zero + enlarge_x(state_one), rhs, zero, 0)
-    out_ref[...] = pressure
+    guess = state_zero + enlarge_x(state_one)
+    sent_guess = begin(guess, 0)
 
     size_x, size_y, _ = facies.shape
     keep_z = (
@@ -262,7 +264,8 @@
         2 * lax.broadcasted_iota(jnp.int32, (size_y // 2, size_y), 0)
         == lax.broadcasted_iota(jnp.int32, (size_y // 2, size_y), 1)
     ).astype(jnp.bfloat16)
-    for channel, field in enumerate((pressure, table_lookup(facies, LOG_PERM_TABLE), source)):
+
+    def put_mean(channel, field):
         mean = (block_sum(field, 1) * 0.125).astype(jnp.bfloat16)
         for plane in range(size_x // 2):
             rows = jnp.dot(keep_y, mean[plane], preferred_element_type=jnp.float32)
@@ -270,6 +273,13 @@
                 rows.astype(jnp.bfloat16), keep_z, preferred_element_type=jnp.float32
             )
             feat_ref[channel, plane] = cells
+
+    put_mean(1, table_lookup(facies, LOG_PERM_TABLE))
+    put_mean(2, source)
+    product = apply_with(guess, finish(sent_guess), zero, 1)
+    pressure = guess + relax_weight * (rhs - product) / zero[2]
+    out_ref[...] = pressure
+    put_mean(0, pressure)
 
 
 def pressure_cycle(facies, pressure_old, column):
@@ -483,15 +493,15 @@
     own[...] = feat_ref[...]
     fill_rims(0, own, far, rows_out, rows_in, fields, row, depth, size_y, size_z)
 
-    @pl.loop(0, size_x + 4)
+    @pl.loop(0, size_x + 4, unroll=2)
     def _(x):
         first[x] = masked(conv(wide, [(0, fields[pl.ds(x, 3)])]), grid, x - 2, size_x)
 
-    @pl.loop(0, size_x + 2)
+    @pl.loop(0, size_x + 2, unroll=2)
     def _(x):
         skip[x] = masked(conv(wide, [(1, first[pl.ds(x, 3)])]), grid, x - 1, size_x)
 
-    @pl.loop(0, pool_x)
+    @pl.loop(0, pool_x, unroll=2)
     def _(x):
         total = skip[2 * x + 1].astype(jnp.float32) + skip[2 * x + 2].astype(jnp.float32)
         lanes = total.shape[1]
@@ -507,11 +517,11 @@
         pool_y, pool_z,
     )
 
-    @pl.loop(0, pool_x + 4)
+    @pl.loop(0, pool_x + 4, unroll=2)
     def _(x):
         middle[x] = masked(conv(wide_pool, [(2, pooled[pl.ds(x, 3)])]), grid_pool, x - 2, pool_x)
 
-    @pl.loop(0, pool_x + 2)
+    @pl.loop(0, pool_x + 2, unroll=2)
     def _(x):
         values = masked(conv(wide_pool, [(3, middle[pl.ds(x, 3)])]), grid_pool, x - 1, pool_x)
         deep[x] = jnp.dot(values, up_ref[...], preferred_element_type=jnp.float32).astype(
@@ -521,7 +531,7 @@
     for x in range(size_x + 2):
         raised[x] = deep[(x + 1) // 2]
 
-    @pl.loop(0, size_x)
+    @pl.loop(0, size_x, unroll=2)
     def _(x):
         values = conv(wide, [(4, skip[pl.ds(x, 3)]), (5, raised[pl.ds(x, 3)])])
         values = values.astype(jnp.bfloat16).astype(jnp.float32)

time: 106 us -> 99.7 us (0.941)
  Pallas kernels: 92.6 us -> 86.5 us
    pallas_call x1, Pallas kernels: 43.7 us -> 38.4 us  [network(): pl.pallas_call(functools.partial(network_kernel, (lax.axis_size('gx'), la...]
where the time goes in v3:
time: 99.7 us; the launch traced here: 99.4 us
  Pallas kernels  86.5 us (87%)
  local copies, waits for them, and re-layouts  8.7 us (9%)
  other arithmetic  2.35 us (2%)
    pallas_call x1, Pallas kernels, pressure_cycle(): pl.pallas_call(functools.partial(cycle_kernel, (lax.axis_size('gx'), lax....  48 us
    pallas_call x1, Pallas kernels, network(): pl.pallas_call(functools.partial(network_kernel, (lax.axis_size('gx'), la...  38.4 us
    unnamed x34, local copies, waits for them, and re-layouts  5.52 us

profile of v3, /device:TPU:0, one launch (start us, length us, event | category | flops | bytes accessed | tf_op | source)
XLA Modules:
  0.0 99.4 jit_solution(8119204932335177065)
XLA Ops:
  0.6 0.7 convert_element_type.6
  1.3 0.9 convolution_bitcast_fusion
  2.2 0.0 copy-start.12
  2.2 0.2 copy.26.col_ref
  2.4 0.0 copy-start.2
  2.4 0.9 copy-done.2
  3.4 0.0 copy-start.3
  3.4 0.9 copy-done.3
  4.3 48.0 %shard_map.167 = (f32[16,32,128]{2,1,0:T(8,128)S(1)}, f32[3,8,16,64]{3,2,1,0:T(8,128)S(1)}) custom-call(s32[16,32,128]{2,1,0:T(8,128)S(1)} %copy-done.2, f32[16,32,128]{2,1,0:T(8,128)S(1)} %copy-done.3, f32[16,32,1]{2,1,0:T(8,128)S(1)} %copy.26.col_ref), custom_call_target="tpu_custom_call" | custom-call | tf_op jit(solution)/shard_map/pallas_call | solution.py:300
  52.4 0.0 copy-start.9
  52.4 0.0 copy-start.10
  52.4 0.0 copy-start.11
  52.4 0.9 convert_bitcast_fusion
  53.4 0.0 copy-start.7
  53.4 0.1 fusion.6
  53.5 0.5 reshape.39
  54.1 0.0 copy-start.13
  54.1 0.0 copy-start
  54.1 0.0 copy-start.4
  54.1 0.0 copy-start.5
  54.1 0.2 pad.13.feat_ref
  54.3 0.0 copy-done.12
  54.3 0.1 copy.28
  54.5 0.1 constant_dynamic-update-slice_fusion
  54.5 0.0 copy-done.9
  54.5 0.1 copy_dynamic-update-slice_fusion.4
  54.6 0.0 copy-done.10
  54.6 0.1 copy_dynamic-update-slice_fusion.3
  54.7 0.0 copy-done.11
  54.7 0.1 copy_dynamic-update-slice_fusion.2
  54.8 0.0 copy-done.7
  54.8 0.1 fusion.17
  54.9 0.1 copy_dynamic-update-slice_fusion.1
  55.0 0.1 copy_dynamic-update-slice_fusion
  55.1 0.0 copy-start.6
  55.1 0.9 copy-done.6
  56.0 1.6 %reshape.37.weight_ref = bf16[6,144,48]{2,1,0:T(8,128)(2,1)S(1)} reshape(bf16[6,9,16,3,16]{4,3,2,1,0:T(4,128)(2,1)} %bitcast.20) | data formatting | bytes 165888 | tf_op jit(solution)/shard_map/reshape | solution.py:357
  57.6 0.0 copy-done.13
  57.6 0.1 copy.34.head_ref
  57.7 0.0 copy-done
  57.7 0.0 copy-done.4
  57.7 0.0 copy-done.5
  57.7 0.0 copy-start.1
  57.7 1.6 %copy-done.1 = bf16[640,1664]{1,0:T(8,128)(2,1)S(1)} copy-done((bf16[640,1664]{1,0:T(8,128)(2,1)S(1)}, bf16[640,1664]{1,0:T(8,128)(2,1)}, u32[]{:S(2)}) %copy-start.1) | copy-done | bytes 2129944
  59.3 0.0 copy-start.8
  59.3 38.4 %shard_map.168 = f32[8,1,1664]{2,1,0:T(1,128)S(1)} custom-call(bf16[8,16,1664]{2,1,0:T(8,128)(2,1)S(1)} %pad.13.feat_ref, bf16[6,144,48]{2,1,0:T(8,128)(2,1)S(1)} %reshape.37.weight_ref, s32[2,1664]{1,0:T(2,128)S(1)} %copy-done.4, s32[2,640]{1,0:T(2,128)S(1)} %copy-done.5, bf16[1664,640]{1,0:T(8,128)(2,1)S(1)} %copy-done, bf16[640,1664]{1,0:T(8,128)(2,1)S(1)} %copy-done.1, ...), custom_call_target="tpu_custom_call" | custom-call | tf_op jit(solution)/shard_map/pallas_call | solution.py:568
  97.8 0.2 slice_reduce_fusion
  98.0 0.1 reshape_squeeze.3
  98.1 0.0 copy-done.8
  98.1 0.6 slice_add_fusion
  98.7 0.7 copy.47
  (6 shorter events, 0.1 us)
Async XLA Ops:
  2.2 52.0 %copy-start.12 = (bf16[16,4,3,3,3]{0,1,4,3,2:T(4,128)(2,1)S(1)}, bf16[16,4,3,3,3]{0,1,4,3,2:T(4,128)(2,1)}, u32[]{:S(2)}) copy-start(bf16[16,4,3,3,3]{0,1,4,3,2:T(4,128)(2,1)} %param.22) | copy-start | bytes 10372
  2.4 1.0 copy-start.2
  3.4 0.9 copy-start.3
  52.4 2.1 %copy-start.9 = (bf16[16,16,3,3,3]{1,0,4,3,2:T(8,128)(2,1)S(1)}, bf16[16,16,3,3,3]{1,0,4,3,2:T(8,128)(2,1)}, u32[]{:S(2)}) copy-start(bf16[16,16,3,3,3]{1,0,4,3,2:T(8,128)(2,1)} %param.23) | copy-start | bytes 41476
  52.4 2.2 %copy-start.10 = (bf16[16,16,3,3,3]{1,0,4,3,2:T(8,128)(2,1)S(1)}, bf16[16,16,3,3,3]{1,0,4,3,2:T(8,128)(2,1)}, u32[]{:S(2)}) copy-start(bf16[16,16,3,3,3]{1,0,4,3,2:T(8,128)(2,1)} %param.24) | copy-start | bytes 41476
  52.4 2.3 %copy-start.11 = (bf16[16,16,3,3,3]{1,0,4,3,2:T(8,128)(2,1)S(1)}, bf16[16,16,3,3,3]{1,0,4,3,2:T(8,128)(2,1)}, u32[]{:S(2)}) copy-start(bf16[16,16,3,3,3]{1,0,4,3,2:T(8,128)(2,1)} %param.25) | copy-start | bytes 41476
  53.4 1.4 %copy-start.7 = (bf16[16,32,3,3,3]{1,0,4,3,2:T(8,128)(2,1)S(1)}, bf16[16,32,3,3,3]{1,0,4,3,2:T(8,128)(2,1)}, u32[]{:S(2)}) copy-start(bf16[16,32,3,3,3]{1,0,4,3,2:T(8,128)(2,1)} %param.26) | copy-start | bytes 82948
  54.1 3.6 %copy-start.13 = (bf16[16]{0:T(256)(128)(2,1)S(1)}, bf16[16]{0:T(256)(128)(2,1)}, u32[]{:S(2)}) copy-start(bf16[16]{0:T(256)(128)(2,1)} %param.27) | copy-start | bytes 100
  54.1 3.7 %copy-start = (bf16[1664,640]{1,0:T(8,128)(2,1)S(1)}, bf16[1664,640]{1,0:T(8,128)(2,1)}, u32[]{:S(2)}) copy-start(bf16[1664,640]{1,0:T(8,128)(2,1)} %constant.28.clone.keep_ref) | copy-start | bytes 6389764
  54.1 3.6 %copy-start.4 = (s32[2,1664]{1,0:T(2,128)S(1)}, s32[2,1664]{1,0:T(2,128)}, u32[]{:S(2)}) copy-start(s32[2,1664]{1,0:T(2,128)} %constant.26.clone.index_ref) | copy-start | bytes 39940
  54.1 3.6 %copy-start.5 = (s32[2,640]{1,0:T(2,128)S(1)}, s32[2,640]{1,0:T(2,128)}, u32[]{:S(2)}) copy-start(s32[2,640]{1,0:T(2,128)} %constant.27.clone.pool_index_ref) | copy-start | bytes 15364
  55.1 0.9 copy-start.6
  57.7 1.6 %copy-start.1 = (bf16[640,1664]{1,0:T(8,128)(2,1)S(1)}, bf16[640,1664]{1,0:T(8,128)(2,1)}, u32[]{:S(2)}) copy-start(bf16[640,1664]{1,0:T(8,128)(2,1)} %constant.29.clone.up_ref) | copy-start | bytes 6389764
  59.3 38.7 %copy-start.8 = (f32[8,16,64]{2,1,0:T(8,128)S(1)}, f32[8,16,64]{2,1,0:T(8,128)}, u32[]{:S(2)}) copy-start(f32[8,16,64]{2,1,0:T(8,128)} %param.18) | copy-start | bytes 98308

commit v4 on v3

--- a/solution.py
+++ b/solution.py
@@ -493,11 +493,11 @@
     own[...] = feat_ref[...]
     fill_rims(0, own, far, rows_out, rows_in, fields, row, depth, size_y, size_z)
 
-    @pl.loop(0, size_x + 4, unroll=2)
+    @pl.loop(0, size_x + 4, unroll=4)
     def _(x):
         first[x] = masked(conv(wide, [(0, fields[pl.ds(x, 3)])]), grid, x - 2, size_x)
 
-    @pl.loop(0, size_x + 2, unroll=2)
+    @pl.loop(0, size_x + 2, unroll=5)
     def _(x):
         skip[x] = masked(conv(wide, [(1, first[pl.ds(x, 3)])]), grid, x - 1, size_x)
 
@@ -531,7 +531,7 @@
     for x in range(size_x + 2):
         raised[x] = deep[(x + 1) // 2]
 
-    @pl.loop(0, size_x, unroll=2)
+    @pl.loop(0, size_x, unroll=4)
     def _(x):
         values = conv(wide, [(4, skip[pl.ds(x, 3)]), (5, raised[pl.ds(x, 3)])])
         values = values.astype(jnp.bfloat16).astype(jnp.float32)

time: 99.7 us -> 98.1 us (0.984)
  Pallas kernels: 86.5 us -> 84.9 us
    pallas_call x1, Pallas kernels: 38.4 us -> 36.9 us  [network(): pl.pallas_call(functools.partial(network_kernel, (lax.axis_size('gx'), la...]
where the time goes in v4:
time: 98.1 us; the launch traced here: 97.8 us
  Pallas kernels  84.9 us (87%)
  local copies, waits for them, and re-layouts  8.7 us (9%)
  other arithmetic  2.35 us (2%)
    pallas_call x1, Pallas kernels, pressure_cycle(): pl.pallas_call(functools.partial(cycle_kernel, (lax.axis_size('gx'), lax....  48 us
    pallas_call x1, Pallas kernels, network(): pl.pallas_call(functools.partial(network_kernel, (lax.axis_size('gx'), la...  36.9 us
    unnamed x34, local copies, waits for them, and re-layouts  5.52 us

profile of v4, /device:TPU:0, one launch (start us, length us, event | category | flops | bytes accessed | tf_op | source)
XLA Modules:
  0.0 97.8 jit_solution(12529898402527816643)
XLA Ops:
  0.6 0.7 convert_element_type.6
  1.3 0.9 convolution_bitcast_fusion
  2.2 0.0 copy-start.12
  2.2 0.2 copy.26.col_ref
  2.4 0.0 copy-start.2
  2.4 0.9 copy-done.2
  3.4 0.0 copy-start.3
  3.4 0.9 copy-done.3
  4.3 48.0 %shard_map.167 = (f32[16,32,128]{2,1,0:T(8,128)S(1)}, f32[3,8,16,64]{3,2,1,0:T(8,128)S(1)}) custom-call(s32[16,32,128]{2,1,0:T(8,128)S(1)} %copy-done.2, f32[16,32,128]{2,1,0:T(8,128)S(1)} %copy-done.3, f32[16,32,1]{2,1,0:T(8,128)S(1)} %copy.26.col_ref), custom_call_target="tpu_custom_call" | custom-call | tf_op jit(solution)/shard_map/pallas_call | solution.py:300
  52.4 0.0 copy-start.9
  52.4 0.0 copy-start.10
  52.4 0.0 copy-start.11
  52.4 0.9 convert_bitcast_fusion
  53.4 0.0 copy-start.7
  53.4 0.1 fusion.6
  53.5 0.5 reshape.39
  54.1 0.0 copy-start.13
  54.1 0.0 copy-start
  54.1 0.0 copy-start.4
  54.1 0.0 copy-start.5
  54.1 0.2 pad.13.feat_ref
  54.3 0.0 copy-done.12
  54.3 0.1 copy.28
  54.5 0.1 constant_dynamic-update-slice_fusion
  54.5 0.0 copy-done.9
  54.5 0.1 copy_dynamic-update-slice_fusion.4
  54.6 0.0 copy-done.10
  54.6 0.1 copy_dynamic-update-slice_fusion.3
  54.7 0.0 copy-done.11
  54.7 0.1 copy_dynamic-update-slice_fusion.2
  54.8 0.0 copy-done.7
  54.8 0.1 fusion.17
  54.9 0.1 copy_dynamic-update-slice_fusion.1
  55.0 0.1 copy_dynamic-update-slice_fusion
  55.1 0.0 copy-start.6
  55.1 0.9 copy-done.6
  56.0 1.6 %reshape.37.weight_ref = bf16[6,144,48]{2,1,0:T(8,128)(2,1)S(1)} reshape(bf16[6,9,16,3,16]{4,3,2,1,0:T(4,128)(2,1)} %bitcast.20) | data formatting | bytes 165888 | tf_op jit(solution)/shard_map/reshape | solution.py:357
  57.6 0.0 copy-done.13
  57.6 0.1 copy.34.head_ref
  57.7 0.0 copy-done
  57.7 0.0 copy-done.4
  57.7 0.0 copy-done.5
  57.7 0.0 copy-start.1
  57.7 1.6 %copy-done.1 = bf16[640,1664]{1,0:T(8,128)(2,1)S(1)} copy-done((bf16[640,1664]{1,0:T(8,128)(2,1)S(1)}, bf16[640,1664]{1,0:T(8,128)(2,1)}, u32[]{:S(2)}) %copy-start.1) | copy-done | bytes 2129944
  59.3 0.0 copy-start.8
  59.3 36.9 %shard_map.168 = f32[8,1,1664]{2,1,0:T(1,128)S(1)} custom-call(bf16[8,16,1664]{2,1,0:T(8,128)(2,1)S(1)} %pad.13.feat_ref, bf16[6,144,48]{2,1,0:T(8,128)(2,1)S(1)} %reshape.37.weight_ref, s32[2,1664]{1,0:T(2,128)S(1)} %copy-done.4, s32[2,640]{1,0:T(2,128)S(1)} %copy-done.5, bf16[1664,640]{1,0:T(8,128)(2,1)S(1)} %copy-done, bf16[640,1664]{1,0:T(8,128)(2,1)S(1)} %copy-done.1, ...), custom_call_target="tpu_custom_call" | custom-call | tf_op jit(solution)/shard_map/pallas_call | solution.py:568
  96.2 0.2 slice_reduce_fusion
  96.4 0.1 reshape_squeeze.3
  96.5 0.0 copy-done.8
  96.5 0.6 slice_add_fusion
  97.1 0.7 copy.47
  (6 shorter events, 0.1 us)
Async XLA Ops:
  2.2 52.0 %copy-start.12 = (bf16[16,4,3,3,3]{0,1,4,3,2:T(4,128)(2,1)S(1)}, bf16[16,4,3,3,3]{0,1,4,3,2:T(4,128)(2,1)}, u32[]{:S(2)}) copy-start(bf16[16,4,3,3,3]{0,1,4,3,2:T(4,128)(2,1)} %param.22) | copy-start | bytes 10372
  2.4 1.0 copy-start.2
  3.4 0.9 copy-start.3
  52.4 2.1 %copy-start.9 = (bf16[16,16,3,3,3]{1,0,4,3,2:T(8,128)(2,1)S(1)}, bf16[16,16,3,3,3]{1,0,4,3,2:T(8,128)(2,1)}, u32[]{:S(2)}) copy-start(bf16[16,16,3,3,3]{1,0,4,3,2:T(8,128)(2,1)} %param.23) | copy-start | bytes 41476
  52.4 2.2 %copy-start.10 = (bf16[16,16,3,3,3]{1,0,4,3,2:T(8,128)(2,1)S(1)}, bf16[16,16,3,3,3]{1,0,4,3,2:T(8,128)(2,1)}, u32[]{:S(2)}) copy-start(bf16[16,16,3,3,3]{1,0,4,3,2:T(8,128)(2,1)} %param.24) | copy-start | bytes 41476
  52.4 2.3 %copy-start.11 = (bf16[16,16,3,3,3]{1,0,4,3,2:T(8,128)(2,1)S(1)}, bf16[16,16,3,3,3]{1,0,4,3,2:T(8,128)(2,1)}, u32[]{:S(2)}) copy-start(bf16[16,16,3,3,3]{1,0,4,3,2:T(8,128)(2,1)} %param.25) | copy-start | bytes 41476
  53.4 1.4 %copy-start.7 = (bf16[16,32,3,3,3]{1,0,4,3,2:T(8,128)(2,1)S(1)}, bf16[16,32,3,3,3]{1,0,4,3,2:T(8,128)(2,1)}, u32[]{:S(2)}) copy-start(bf16[16,32,3,3,3]{1,0,4,3,2:T(8,128)(2,1)} %param.26) | copy-start | bytes 82948
  54.1 3.6 %copy-start.13 = (bf16[16]{0:T(256)(128)(2,1)S(1)}, bf16[16]{0:T(256)(128)(2,1)}, u32[]{:S(2)}) copy-start(bf16[16]{0:T(256)(128)(2,1)} %param.27) | copy-start | bytes 100
  54.1 3.7 %copy-start = (bf16[1664,640]{1,0:T(8,128)(2,1)S(1)}, bf16[1664,640]{1,0:T(8,128)(2,1)}, u32[]{:S(2)}) copy-start(bf16[1664,640]{1,0:T(8,128)(2,1)} %constant.28.clone.keep_ref) | copy-start | bytes 6389764
  54.1 3.6 %copy-start.4 = (s32[2,1664]{1,0:T(2,128)S(1)}, s32[2,1664]{1,0:T(2,128)}, u32[]{:S(2)}) copy-start(s32[2,1664]{1,0:T(2,128)} %constant.26.clone.index_ref) | copy-start | bytes 39940
  54.1 3.6 %copy-start.5 = (s32[2,640]{1,0:T(2,128)S(1)}, s32[2,640]{1,0:T(2,128)}, u32[]{:S(2)}) copy-start(s32[2,640]{1,0:T(2,128)} %constant.27.clone.pool_index_ref) | copy-start | bytes 15364
  55.1 0.9 copy-start.6
  57.7 1.6 %copy-start.1 = (bf16[640,1664]{1,0:T(8,128)(2,1)S(1)}, bf16[640,1664]{1,0:T(8,128)(2,1)}, u32[]{:S(2)}) copy-start(bf16[640,1664]{1,0:T(8,128)(2,1)} %constant.29.clone.up_ref) | copy-start | bytes 6389764
  59.3 37.1 %copy-start.8 = (f32[8,16,64]{2,1,0:T(8,128)S(1)}, f32[8,16,64]{2,1,0:T(8,128)}, u32[]{:S(2)}) copy-start(f32[8,16,64]{2,1,0:T(8,128)} %param.18) | copy-start | bytes 98308
